TPU v7x, 128 devices: a whole 4x4x4 slice. The times are simulated.
128 devices in a mesh: group: 8 (over y, core), sub: 16 (over z, x).
Axes of the slice: x: 4, y: 4, z: 4, core: 2. Of those that a mesh axis runs over, the one named last changes fastest.
Arguments:
- current: float32 [16, 786432], P(None, ('group', 'sub')), may hold values from -6 to 6
- previous: float32 [16, 786432], P(None, ('group', 'sub')), may hold values from -6 to 6
- prev_coupling: float32 [16, 16], replicated, may hold values from -3 to 3
- mass_diag: float32 [786432], P(('group', 'sub')), may hold values from 1 to 2
- near_blocks: bfloat16 [6144, 8, 128, 128], P(('group', 'sub')), may hold values from -0.1875 to 0.1875
- near_cols: int32 [6144, 8], P(('group', 'sub')), may hold values from 0 to 6143, as said below
- cluster_basis: bfloat16 [6144, 24, 128], P(('group', 'sub')), may hold values from -0.5 to 0.5
- coupling: bfloat16 [6144, 24, 768], P(('group', 'sub')), may hold values from -0.21875 to 0.21875
- send_list: int32 [128, 128, 12], P(('group', 'sub')), may hold values from -1 to 47, as said below
- far_slot: int32 [6144, 32], P(('group', 'sub')), may hold values from 0 to 1535, as said below
Outputs:
- next_block: float32 [16, 786432], P(None, ('group', 'sub'))
- projection: float32 [16, 16], replicated
- triangle: float32 [16, 16], replicated
Inputs may be any that keep to these rules, and one draw needn't show every extreme that they name: near_cols[r, 0] = r; the other near column clusters of a row are distinct, differ from r, and lie on the row cluster's device or on the devices just before or after it in the order of group then sub, taken round the ends. `send_list`: for each source and destination the live slots come first, 1 to 12 of them; every source fills all 12 slots for one destination. `far_slot`: each entry names a live slot that its source sends to the row cluster's device.
All inputs are finite; a program needn't handle non-finite values.
Results may differ from a plain program's by a relative error of at most 0.002.
Values may be sent and summed in bfloat16 or wider, within the bound.
A program may use at most 128 MiB of HBM per device.

v0:
```python
import jax
import jax.numpy as jnp
from jax import lax
from jax.sharding import PartitionSpec as P

CL = 128
RANK = 24
NFAR = 32
CAP = 12


def with_halo(x, sides, width):
    for axis, dim in sides:
        devices, length = (lax.axis_size(axis), x.shape[dim])
        up = [(i, (i + 1) % devices) for i in range(devices)]
        down = [(j, i) for i, j in up]
        last = lax.slice_in_dim(x, length - width, length, axis=dim)
        leading = lax.slice_in_dim(x, 0, width, axis=dim)
        before = lax.ppermute(last, axis, up)
        after = lax.ppermute(leading, axis, down)
        x = jnp.concatenate([before, x, after], axis=dim)
    return x


def pack_slots(coefficients, send_list):
    slot_ids = send_list[0]
    chosen = coefficients[jnp.maximum(slot_ids, 0)]
    return jnp.where((slot_ids >= 0)[:, :, None], chosen, 0.0)


def per_device(
    current,
    previous,
    prev_coupling,
    mass_diag,
    near_blocks,
    near_cols,
    cluster_basis,
    coupling,
    send_list,
    far_slot,
):
    highest = lax.Precision.HIGHEST
    rhs_count, row_count = current.shape
    clusters = row_count // CL
    devices = lax.axis_size(("group", "sub"))
    device = lax.axis_index(("group", "sub"))
    current_lo = current.astype(jnp.bfloat16)
    blocks = current_lo.reshape(rhs_count, clusters, CL)
    coefficients = jnp.einsum(
        "ckb,scb->cks", cluster_basis, blocks, preferred_element_type=jnp.float32
    )
    coefficients = coefficients.reshape(clusters, RANK * rhs_count)
    feature = coefficients.shape[1]
    packed = pack_slots(coefficients, send_list)
    arrived = lax.all_to_all(packed, ("group", "sub"), split_axis=0, concat_axis=0, tiled=True)
    picked = arrived.reshape(devices * CAP, feature)[far_slot]
    picked = picked.reshape(clusters, NFAR * RANK, rhs_count)
    combined = jnp.einsum("rkm,rms->rks", coupling.astype(jnp.float32), picked, precision=highest)
    far_part = jnp.einsum(
        "rka,rks->sra",
        cluster_basis,
        combined.astype(jnp.bfloat16),
        preferred_element_type=jnp.float32,
    )
    far_part = far_part.reshape(rhs_count, row_count)
    window = with_halo(current_lo, ((("group", "sub"), 1),), row_count)
    window_ids = (near_cols - (device - 1) * clusters) % (devices * clusters)
    gathered = window.reshape(rhs_count, 3 * clusters, CL)[:, window_ids]
    near_part = jnp.einsum(
        "rjab,srjb->sra", near_blocks, gathered, preferred_element_type=jnp.float32
    )
    near_part = near_part.reshape(rhs_count, row_count)
    image = near_part + far_part + mass_diag[None, :] * current
    total = float(devices * row_count)
    projection = lax.psum(jnp.dot(current, image.T, precision=highest), ("group", "sub")) / total
    resid = (
        image
        - jnp.dot(projection.T, current, precision=highest)
        - jnp.dot(prev_coupling, previous, precision=highest)
    )
    gram = lax.psum(jnp.dot(resid, resid.T, precision=highest), ("group", "sub")) / total
    triangle = jnp.linalg.cholesky(gram)
    next_block = lax.linalg.triangular_solve(triangle, resid, left_side=True, lower=True)
    return (next_block, projection, triangle)


def solution(mesh):
    placed = (
        P(None, ("group", "sub")),
        P(None, ("group", "sub")),
        P(),
        P(("group", "sub")),
        P(("group", "sub"), None, None, None),
        P(("group", "sub"), None),
        P(("group", "sub"), None, None),
        P(("group", "sub"), None, None),
        P(("group", "sub"), None, None),
        P(("group", "sub"), None),
    )
    return jax.shard_map(
        per_device,
        mesh=mesh,
        in_specs=placed,
        out_specs=(P(None, ("group", "sub")), P(), P()),
        check_vma=False,
    )
```

profile of v0, /device:TPU:0, one launch (start us, length us, event | category | flops | bytes accessed | tf_op | source)
XLA Modules:
  0.0 261.8 jit_solution(14668627590266075201)
XLA Ops:
  0.6 0.0 copy-start
  0.6 0.8 broadcast_maximum_fusion
  1.5 0.7 broadcast_compare_fusion
  2.2 1.3 fusion.2
  3.5 0.2 copy.34
  3.8 0.1 copy.36
  3.9 0.1 copy.35
  4.0 0.1 reshape.68
  4.1 4.8 %gather_fusion.1 = f32[1536,384]{1,0:T(8,128)} fusion(f32[48,384]{1,0:T(8,128)S(1)} %copy.36, s32[2048]{0:T(1024)S(1)} %pad_clamp_fusion.1), kind=kCustom, calls=%fused_computation.1 | custom fusion | bytes 4724736 | tf_op jit(solution)/shard_map/gather | solution.py:27
  8.9 3.7 %reshape.67 = f32[128,12,384]{2,1,0:T(8,128)} reshape(f32[1536,384]{1,0:T(8,128)} %gather_fusion.1) | data formatting | bytes 4718592 | tf_op jit(solution)/shard_map/gather | solution.py:27
  12.6 0.1 copy.46
  12.8 3.3 %broadcast_select_fusion = f32[128,12,384]{2,1,0:T(8,128)} fusion(f32[128,12,384]{2,1,0:T(8,128)} %reshape.67, pred[128,12]{1,0:T(8,128)(4,1)S(1)} %bitcast.59), kind=kLoop, calls=%fused_computation.5 | loop fusion | flops 589824 | bytes 4720128 | tf_op jit(solution)/shard_map/jit(_where)/select_n | solution.py:28
  16.1 0.0 copy-start.1
  16.1 0.0 copy-start.5
  16.1 0.0 copy-start.7
  16.1 11.6 %all-to-all-start = ((f32[128,12,384]{2,1,0:T(8,128)}), f32[128,12,384]{2,1,0:T(8,128)}, u32[]{:S(2)}, u32[]{:S(2)}) async-start(f32[128,12,384]{2,1,0:T(8,128)} %broadcast_select_fusion), calls=%async_computation | async-start | bytes 6291456 | tf_op jit(solution)/shard_map/all_to_all | solution.py:56
  27.7 0.0 copy-done.1
  27.7 7.1 %collective-permute-start.1 = (bf16[16,6144]{1,0:T(8,128)(2,1)S(1)}, bf16[16,6144]{1,0:T(8,128)(2,1)S(1)}, u32[]{:S(2)}, u32[]{:S(2)}) collective-permute-start(bf16[16,6144]{1,0:T(8,128)(2,1)S(1)} %convert_element_type.8), channel_id=1, source_target_pairs={{1,0},{2,1},{3,2},{4,3},{5,4},{6,5},{7,6},{8,7},{9,8},{10,9},{11,1... | collective-permute-start | bytes 589832 | tf_op jit(solution)/shard_map/ppermute | solution.py:20
  34.8 0.0 collective-permute-start
  34.8 0.0 copy-done.5
  34.8 0.1 copy.37
  34.9 0.1 reshape.76
  35.0 0.0 copy-done.7
  35.0 0.1 copy.30
  35.1 0.1 reshape.60
  35.2 31.3 %collective-permute-done.1 = bf16[16,6144]{1,0:T(8,128)(2,1)S(1)} collective-permute-done((bf16[16,6144]{1,0:T(8,128)(2,1)S(1)}, bf16[16,6144]{1,0:T(8,128)(2,1)S(1)}, u32[]{:S(2)}, u32[]{:S(2)}) %collective-permute-start.1) | collective-permute-done | bytes 196640 | tf_op jit(solution)/shard_map/ppermute | solution.py:20
  66.4 5.9 %collective-permute-done = bf16[16,6144]{1,0:T(8,128)(2,1)S(1)} collective-permute-done((bf16[16,6144]{1,0:T(8,128)(2,1)S(1)}, bf16[16,6144]{1,0:T(8,128)(2,1)S(1)}, u32[]{:S(2)}, u32[]{:S(2)}) %collective-permute-start) | collective-permute-done | bytes 196640 | tf_op jit(solution)/shard_map/ppermute | solution.py:19
  72.3 0.1 copy_bitcast_fusion
  72.4 2.6 gather_fusion
  75.0 0.0 all-to-all-done
  75.0 4.0 %reshape.56 = f32[1536,384]{1,0:T(8,128)} reshape(f32[128,12,384]{2,1,0:T(8,128)} %all-to-all-done) | data formatting | bytes 4718592 | tf_op jit(solution)/shard_map/reshape | solution.py:57
  79.0 6.9 %gather_fusion.2 = f32[1536,384]{1,0:T(8,128)} fusion(f32[1536,384]{1,0:T(8,128)} %reshape.56, s32[2048]{0:T(1024)S(1)} %pad_clamp_fusion), kind=kCustom, calls=%fused_computation.2 | custom fusion | bytes 4724736 | tf_op jit(solution)/shard_map/gather | solution.py:57
  85.8 12.0 %reshape.57 = f32[48,768,16]{2,1,0:T(8,128)} reshape(f32[1536,384]{1,0:T(8,128)} %gather_fusion.2) | data formatting | bytes 4718592 | tf_op jit(solution)/shard_map/reshape | solution.py:58
  97.8 0.0 copy-done
  97.8 0.0 copy-start.2
  97.8 21.1 %convolution_convert_fusion = bf16[48,16,24]{2,1,0:T(8,128)(2,1)S(1)} fusion(f32[48,768,16]{2,1,0:T(8,128)} %reshape.57, bf16[48,24,768]{2,1,0:T(8,128)(2,1)S(1)} %copy-done), kind=kOutput, calls=%fused_computation.9 | convolution fusion | flops 169887744 | bytes 4165632 | tf_op jit(solution)/shard_map/rkm,rms->rks/dot_general | solution.py:59
  119.0 0.0 copy-done.2
  119.0 0.3 fusion.9
  119.2 0.0 copy-start.4
  119.3 8.4 %fusion.1 = f32[48,2,8,128]{3,2,1,0:T(8,128)S(1)} fusion(f32[48,16,128]{2,1,0:T(8,128)S(1)} %fusion.9, bf16[16,48,8,128]{3,0,2,1:T(8,128)(2,1)} %bitcast.57, bf16[48,8,128,128]{3,2,1,0:T(8,128)(2,1)} %param.14), kind=kOutput, calls=%fused_computation.8 | convolution fusion | flops 201424896 | bytes 14942208 | tf_op jit(solution)/shard_map/rjab,srjb->sra/dot_general | solution.py:70
  127.7 0.0 copy-done.4
  127.7 0.0 copy-start.3
  127.7 0.0 copy-start.6
  127.7 0.8 convolution_bitcast_fusion.1
  128.6 62.8 %psum.14 = f32[16,16]{0,1:T(8,128)S(1)} all-reduce(f32[16,16]{0,1:T(8,128)S(1)} %convolution_bitcast_fusion.1), channel_id=1, replica_groups=mesh['group'=8,'sub'=16] {'group','sub'}, use_global_device_ids=true, to_apply=%region_0.1 | all-reduce | flops 256 | bytes 2048 | tf_op jit(solution)/shard_map/psum | solution.py:76
  191.3 0.5 convolution_subtract_fusion.1
  191.8 0.0 copy-done.3
  191.8 0.0 copy-done.6
  191.8 0.5 convolution_subtract_fusion
  192.3 0.6 fusion.10
  192.9 62.2 %psum.15 = f32[16,16]{0,1:T(8,128)S(1)} all-reduce(f32[16,16]{0,1:T(8,128)S(1)} %fusion.10), channel_id=1, replica_groups=mesh['group'=8,'sub'=16] {'group','sub'}, use_global_device_ids=true, to_apply=%region_1.2 | all-reduce | flops 256 | bytes 2048 | tf_op jit(solution)/shard_map/psum | solution.py:82
  255.2 0.1 copy.41
  255.2 1.5 cholesky.16
  256.7 0.6 compare_reduce_fusion
  257.4 1.2 select_bitcast_fusion
  258.6 1.2 custom-call.6
  259.8 1.3 fusion.6
  261.1 0.7 copy.42
  (10 shorter events, 0.1 us)
Async XLA Ops:
  0.6 97.2 %copy-start = (bf16[48,24,768]{2,1,0:T(8,128)(2,1)S(1)}, bf16[48,24,768]{2,1,0:T(8,128)(2,1)}, u32[]{:S(2)}) copy-start(bf16[48,24,768]{2,1,0:T(8,128)(2,1)} %param.17) | copy-start | bytes 5308420
  16.1 11.6 %copy-start.1 = (f32[16,6144]{1,0:T(8,128)S(1)}, f32[16,6144]{1,0:T(8,128)}, u32[]{:S(2)}) copy-start(f32[16,6144]{1,0:T(8,128)} %param.10) | copy-start | bytes 1179652
  16.1 18.7 %copy-start.5 = (s32[48,32]{0,1:T(8,128)S(1)}, s32[48,32]{0,1:T(8,128)}, u32[]{:S(2)}) copy-start(s32[48,32]{0,1:T(8,128)} %param.19) | copy-start | bytes 18436
  16.1 18.9 %copy-start.7 = (s32[48,8]{0,1:T(8,128)S(1)}, s32[48,8]{0,1:T(8,128)}, u32[]{:S(2)}) copy-start(s32[48,8]{0,1:T(8,128)} %param.15) | copy-start | bytes 4612
  16.1 58.9 %all-to-all-start = ((f32[128,12,384]{2,1,0:T(8,128)}), f32[128,12,384]{2,1,0:T(8,128)}, u32[]{:S(2)}, u32[]{:S(2)}) async-start(f32[128,12,384]{2,1,0:T(8,128)} %broadcast_select_fusion), calls=%async_computation | async-start | bytes 6291456 | tf_op jit(solution)/shard_map/all_to_all | solution.py:56
  27.7 38.7 %collective-permute-start.1 = (bf16[16,6144]{1,0:T(8,128)(2,1)S(1)}, bf16[16,6144]{1,0:T(8,128)(2,1)S(1)}, u32[]{:S(2)}, u32[]{:S(2)}) collective-permute-start(bf16[16,6144]{1,0:T(8,128)(2,1)S(1)} %convert_element_type.8), channel_id=1, source_target_pairs={{1,0},{2,1},{3,2},{4,3},{5,4},{6,5},{7,6},{8,7},{9,8},{10,9},{11,1... | collective-permute-start | bytes 589832 | tf_op jit(solution)/shard_map/ppermute | solution.py:20
  34.8 37.5 %collective-permute-start = (bf16[16,6144]{1,0:T(8,128)(2,1)S(1)}, bf16[16,6144]{1,0:T(8,128)(2,1)S(1)}, u32[]{:S(2)}, u32[]{:S(2)}) collective-permute-start(bf16[16,6144]{1,0:T(8,128)(2,1)S(1)} %convert_element_type.8), channel_id=1, source_target_pairs={{0,1},{1,2},{2,3},{3,4},{4,5},{5,6},{6,7},{7,8},{8,9},{9,10},{10,1... | collective-permute-start | bytes 589832 | tf_op jit(solution)/shard_map/ppermute | solution.py:19
  97.8 21.2 %copy-start.2 = (bf16[48,24,128]{2,1,0:T(8,128)(2,1)S(1)}, bf16[48,24,128]{2,1,0:T(8,128)(2,1)}, u32[]{:S(2)}) copy-start(bf16[48,24,128]{2,1,0:T(8,128)(2,1)} %param.16) | copy-start | bytes 884740
  119.2 8.4 %copy-start.4 = (f32[6144]{0:T(1024)S(1)}, f32[6144]{0:T(1024)}, u32[]{:S(2)}) copy-start(f32[6144]{0:T(1024)} %param.13) | copy-start | bytes 73732
  127.7 64.1 %copy-start.3 = (f32[16,6144]{1,0:T(8,128)S(1)}, f32[16,6144]{1,0:T(8,128)}, u32[]{:S(2)}) copy-start(f32[16,6144]{1,0:T(8,128)} %param.11) | copy-start | bytes 1179652
  127.7 64.1 %copy-start.6 = (f32[16,16]{1,0:T(8,128)S(1)}, f32[16,16]{1,0:T(8,128)}, u32[]{:S(2)}) copy-start(f32[16,16]{1,0:T(8,128)} %param.12) | copy-start | bytes 3076
where the time goes:
time: 263 us; the launch traced here: 262 us
  blocking collectives  125 us (48%)
  waiting for transfers between devices  37.1 us (14%)
  local copies, waits for them, and re-layouts  35.7 us (14%)
  matrix products  34.9 us (13%)
  starting transfers between devices  18.7 us (7%)
  other arithmetic  9.61 us (4%)
    psum x1, blocking collectives, per_device(): lax.psum(jnp.dot(current, image.T, precision=highest), ('group', 'sub'))  62.8 us
    psum x1, blocking collectives, per_device(): lax.psum(jnp.dot(resid, resid.T, precision=highest), ('group', 'sub'))  62.2 us
    ppermute x1, waiting for transfers between devices, with_halo(): after = lax.ppermute(leading, axis, down)  31.3 us
    dot_general x1, matrix products, per_device(): jnp.einsum('rkm,rms->rks', coupling.astype(jnp.float32), picked, precisio...  21.1 us
    reshape x1, local copies, waits for them, and re-layouts, per_device(): picked = picked.reshape(clusters, NFAR * RANK, rhs_count)  12 us
    all_to_all x1, starting transfers between devices, per_device(): lax.all_to_all(packed, ('group', 'sub'), split_axis=0, concat_axis=0, til...  11.6 us
    gather x2, local copies, waits for them, and re-layouts, pack_slots(): chosen = coefficients[jnp.maximum(slot_ids, 0)]  8.5 us
    dot_general x1, matrix products, per_device(): jnp.einsum('rjab,srjb->sra', near_blocks, gathered, preferred_element_typ...  8.44 us
  transfers between devices with their start and end apart: 3, of which 2 were waited for; matrix products, arithmetic and copies ran while one was open for 1% of the time, Pallas kernels for 0%

commit v1 on v0

v1 whole, which is shorter than its diff:
```python
import functools

import jax
import jax.numpy as jnp
from jax import lax
from jax.experimental import pallas as pl
from jax.experimental.pallas import tpu as pltpu
from jax.sharding import PartitionSpec as P

MESH = pl.DeviceIdType.MESH
BF = jnp.bfloat16
F32 = jnp.float32
NRHS = 16
CL = 128
RANK = 24
NNEAR = 8
NFAR = 32
CAP = 12
CPD = 48
NCL = 6144
N = 786432
ROWS = CPD * CL
NGRP = CPD // 8
HIGHEST = lax.Precision.HIGHEST
PART_ROWS = (64, 64, 32)
ORDERS = ((0, 1, 2), (2, 0, 1), (1, 2, 0))
OFFSETS = (2, 1, 3)
NEAR_CHUNKS = 6


def nt(a, b, precision=None):
    return lax.dot_general(
        a, b, (((1,), (1,)), ((), ())), preferred_element_type=F32, precision=precision
    )


def tn(a, b, precision=None):
    return lax.dot_general(
        a, b, (((0,), (0,)), ((), ())), preferred_element_type=F32, precision=precision
    )


def nn(a, b, precision=None):
    return lax.dot_general(
        a, b, (((1,), (0,)), ((), ())), preferred_element_type=F32, precision=precision
    )


def split(x):
    hi = x.astype(BF)
    return hi, (x - hi.astype(F32)).astype(BF)


def kernel(
    cur_h, prev_h, pc_ref, mass_h, near_h, ncol_ref, basis_h, coup_h, slist_ref, far_ref,
    out_ref, proj_ref, tri_ref,
    cur_v, prev_v, mass_v, near_v, basis_v, coup_v,
    win, stack, jbuf, parts_a, parts_b, parts_c, table, xbuf,
    ncol_v, far_v, addr_v, ncol_s, far_s, addr_s,
    red_c, red_t,
    load_sem, near_sem, smem_sem,
    ag_send, ag_recv, sib_send, sib_recv, halo_send, halo_recv, red_send, red_recv,
):
    grp = lax.axis_index("group")
    sub = lax.axis_index("sub")
    me = grp * 16 + sub
    core = grp % 2
    pos = (sub % 4, grp // 2, sub // 4)

    def place(x, y, z, c):
        return (y * 2 + c, z * 4 + x)

    def shifted(axis, off):
        at = list(pos)
        at[axis] = (at[axis] + off) % 4
        return place(*at, core)

    sibling = place(*pos, 1 - core)

    def neighbour(off):
        d = (me + off) % 128
        return (d // 16, d % 16)

    loads = []
    for n, (src, dst) in enumerate(
        ((cur_h, cur_v), (basis_h, basis_v), (prev_h, prev_v), (mass_h, mass_v), (coup_h, coup_v))
    ):
        copy = pltpu.make_async_copy(src, dst, load_sem.at[n])
        copy.start()
        loads.append(copy)
    per = CPD * NNEAR // NEAR_CHUNKS
    near_loads = []
    for n in range(NEAR_CHUNKS):
        part = pl.ds(n * per, per)
        copy = pltpu.make_async_copy(near_h.at[part], near_v.at[part], near_sem.at[n])
        copy.start()
        near_loads.append(copy)

    peers = [shifted(a, o) for a in range(3) for o in OFFSETS]
    peers += [sibling, neighbour(1), neighbour(127)]
    barrier = pltpu.get_barrier_semaphore()
    for d in peers:
        pl.semaphore_signal(barrier, inc=1, device_id=d, device_id_type=MESH)

    wanted = ncol_ref[...] - (me - 1) * CPD
    wanted = jnp.where(wanted < 0, wanted + NCL, wanted)
    wanted = jnp.where(wanted >= NCL, wanted - NCL, wanted)
    ncol_v[:, 0:CPD] = jnp.clip(wanted, 0, 3 * CPD - 1)
    q = far_ref[...]
    src = (q * 43691) >> 19
    slot = q - src * CAP
    src_g, src_s = src >> 4, src & 15
    order = (src_g & 1) * 64 + (src_s & 3) * 16 + (src_s >> 2) * 4 + (src_g >> 1)
    far_v[:, 0:CPD] = jnp.clip(order * 16 + slot, 0, 2047)
    ncol_copy = pltpu.make_async_copy(ncol_v, ncol_s, smem_sem.at[0])
    far_copy = pltpu.make_async_copy(far_v, far_s, smem_sem.at[1])
    ncol_copy.start()
    far_copy.start()

    loads[0].wait()

    def window_step(c, _):
        cols = pl.ds(pl.multiple_of(c * CL, CL), CL)
        hi, lo = split(cur_v[:, cols])
        win[CPD + c] = hi
        stack[32:48, cols] = hi
        stack[48:64, cols] = lo
        return 0

    lax.fori_loop(0, CPD, window_step, 0, unroll=4)
    loads[1].wait()
    diag = lax.broadcasted_iota(jnp.int32, (8 * RANK, 128), 0) // RANK == (
        lax.broadcasted_iota(jnp.int32, (8 * RANK, 128), 1) // NRHS
    )
    coefs = []
    for g in range(NGRP):
        cl = win[CPD + 8 * g : CPD + 8 * g + 8].reshape(128, CL)
        y = nt(basis_v[192 * g : 192 * g + 192, :], cl)
        y = jnp.where(diag, y, 0.0).reshape(8, RANK, 128)
        coefs.append(jnp.sum(y, axis=0))
    coefs = jnp.concatenate(coefs, axis=0).astype(BF)
    slist = jnp.concatenate([slist_ref[...].astype(F32), jnp.zeros((4, 128), F32)], axis=0)
    slist = slist.astype(BF)
    bufs = (parts_a, parts_b, parts_c)

    def block(p, phase, off):
        at = [pos[a] for a in ORDERS[p]]
        at[phase] = (at[phase] + off) % 4
        return bufs[p].at[(core, at[2], at[1], at[0])[: 4 - phase]]

    own = [tuple(pos[a] for a in ORDERS[p]) for p in range(3)]
    i1, i2, i3 = own[0]
    parts_a[core, i3, i2, i1] = coefs[0:64]
    i1, i2, i3 = own[1]
    parts_b[core, i3, i2, i1] = coefs[64:128]
    i1, i2, i3 = own[2]
    parts_c[core, i3, i2, i1] = jnp.concatenate([coefs[128:144], slist], axis=0)

    pl.semaphore_wait(barrier, len(peers))

    sends = []

    def put(src_ref, dst_ref, send_sem, recv_sem, device):
        copy = pltpu.make_async_remote_copy(
            src_ref=src_ref, dst_ref=dst_ref, send_sem=send_sem, recv_sem=recv_sem,
            device_id=device, device_id_type=MESH,
        )
        copy.start()
        sends.append(copy)
        return copy

    def gather_phase(phase):
        copies = []
        for k, off in enumerate(OFFSETS):
            for p in range(3):
                n = (phase * 3 + p) * 3 + k
                ref = block(p, phase, 0)
                copies.append(
                    put(ref, ref, ag_send.at[n], ag_recv.at[n], shifted(ORDERS[p][phase], off))
                )
        return copies

    sib_copies = []

    def to_sibling(ref):
        n = len(sib_copies)
        sib_copies.append(put(ref, ref, sib_send.at[n], sib_recv.at[n], sibling))

    phase1 = gather_phase(0)
    mid = win.at[pl.ds(CPD, CPD)]
    halo = [
        put(mid, win.at[pl.ds(0, CPD)], halo_send.at[0], halo_recv.at[0], neighbour(1)),
        put(mid, win.at[pl.ds(2 * CPD, CPD)], halo_send.at[1], halo_recv.at[1], neighbour(127)),
    ]
    loads[2].wait()
    pc = pc_ref[...]
    pc_hi, pc_lo = split(pc)
    pc_rows = jnp.concatenate([pc_hi, pc_hi], axis=1)
    pc_rows2 = jnp.concatenate([pc_lo, pc_lo], axis=1)
    pc_all = jnp.concatenate([pc_rows, pc_rows2], axis=0)

    def previous_step(c, _):
        cols = pl.ds(pl.multiple_of(c * 512, 512), 512)
        hi, lo = split(prev_v[:, cols])
        stack[64:80, cols] = hi
        stack[80:96, cols] = lo
        both = nn(pc_all, jnp.concatenate([hi, lo], axis=0))
        jbuf[:, cols] = -(both[0:16] + both[16:32])
        return 0

    lax.fori_loop(0, ROWS // 512, previous_step, 0)

    for copy in phase1:
        copy.wait_recv()
    phase2 = gather_phase(1)
    loads[3].wait()
    loads[4].wait()
    for copy in phase2:
        copy.wait_recv()
    phase3 = gather_phase(2)
    for p in range(3):
        to_sibling(block(p, 2, 0))

    ncol_copy.wait()
    for copy in halo:
        copy.wait_recv()

    def near_step(r, _):
        xs, ms = [], []
        for j in range(NNEAR):
            w = ncol_s[j, r]
            xs.append(win[w])
        x = jnp.concatenate(xs, axis=1)
        m = near_v[pl.ds(r * NNEAR, NNEAR)]
        m = jnp.concatenate([m[j] for j in range(NNEAR)], axis=1)
        cols = pl.ds(pl.multiple_of(r * CL, CL), CL)
        jbuf[:, cols] += nt(x, m) + mass_v[pl.ds(r, 1), :] * cur_v[:, cols]
        return 0

    rows_per = CPD // NEAR_CHUNKS
    for n in range(NEAR_CHUNKS):
        near_loads[n].wait()
        lax.fori_loop(n * rows_per, (n + 1) * rows_per, near_step, 0)

    for copy in phase3:
        copy.wait_recv()
    for p in range(3):
        for off in (1, 2, 3):
            to_sibling(block(p, 2, off))
    far_copy.wait()
    for copy in sib_copies:
        copy.wait_recv()

    def table_step(t, _):
        c, x, z, y = t // 64, t // 16 % 4, t // 4 % 4, t % 4
        table[pl.ds(t * 18, 8)] = parts_a[c, z, y, x].astype(F32).reshape(8, 8, 128)
        table[pl.ds(t * 18 + 8, 8)] = parts_b[c, y, x, z].astype(F32).reshape(8, 8, 128)
        table[pl.ds(t * 18 + 16, 2)] = parts_c[c, x, z, y, 0:16].astype(F32).reshape(2, 8, 128)
        return 0

    lax.fori_loop(0, 128, table_step, 0)

    lists = parts_c[:, :, :, :, 16:32].reshape(128 * 16, 128)
    mine = (lax.broadcasted_iota(jnp.int32, (16, 128), 1) == me).astype(BF)
    local = nt(mine, lists)
    row_id = lax.broadcasted_iota(jnp.int32, (16, 128), 0)
    lane_id = lax.broadcasted_iota(jnp.int32, (16, 128), 1)
    picked = jnp.zeros((16, 128), F32)
    for i in range(16):
        picked = jnp.where(row_id == i, local[:, i * 128 : (i + 1) * 128], picked)
    picked = jnp.clip(picked.astype(jnp.int32), 0, CPD - 1)
    first = (row_id * 8 + (lane_id >> 4)) * 18 + (picked >> 3) * 3
    addr_v[...] = jnp.clip(first * 8 + (picked & 7), 0, (128 * 18 - 3) * 8 + 7)
    addr_copy = pltpu.make_async_copy(addr_v, addr_s, smem_sem.at[2])
    addr_copy.start()
    addr_copy.wait()

    lane_block = lax.broadcasted_iota(jnp.int32, (RANK, 128), 1) // NRHS

    def far_step(g, _):
        def pick_step(jj, _):
            halves = []
            for k in range(2):
                total = None
                for r in range(8):
                    at = far_s[jj * 2 + k, g * 8 + r]
                    word = addr_s[at >> 7, at & 127]
                    rows = table[pl.ds(word >> 3, 3)].reshape(RANK, 128)
                    rows = pltpu.roll(rows, ((r - word) & 7) * NRHS, 1)
                    total = rows if r == 0 else jnp.where(lane_block == r, rows, total)
                halves.append(total)
            both = jnp.concatenate(halves, axis=0).astype(BF)
            xbuf[pl.ds(pl.multiple_of(jj * 48, 48), 48), :] = both
            return 0

        lax.fori_loop(0, NFAR // 2, pick_step, 0)
        rows = pl.ds(pl.multiple_of(g * 192, 192), 192)
        combined = nn(coup_v[rows, :], xbuf[...])
        combined = jnp.where(diag, combined, 0.0).astype(BF)
        far = tn(combined, basis_v[rows, :])
        for r in range(8):
            cols = pl.ds(pl.multiple_of((g * 8 + r) * CL, CL), CL)
            val = jbuf[:, cols] + far[r * 16 : r * 16 + 16]
            hi, lo = split(val)
            stack[0:16, cols] = hi
            stack[16:32, cols] = lo
        return 0

    lax.fori_loop(0, NGRP, far_step, 0)

    def inner_step(c, total):
        cols = pl.ds(pl.multiple_of(c * 1024, 1024), 1024)
        s = stack[:, cols]
        return total + nt(s[0:64], s)

    inner = lax.fori_loop(0, ROWS // 1024, inner_step, jnp.zeros((64, 96), F32))
    inner = jnp.concatenate([inner, jnp.zeros((64, 32), F32)], axis=1)
    inner = inner + pltpu.roll(inner, 112, 1)
    j_rows = inner[0:16] + inner[16:32]
    c_rows = pltpu.roll(inner[32:48] + inner[48:64], 16, 1)
    odd = (lane_id // 16) % 2 == 1
    mixed = jnp.where(odd, c_rows, j_rows)

    red_c[core] = mixed
    copy = put(red_c.at[core], red_c.at[core], red_send.at[0], red_recv.at[0], sibling)
    copy.wait_recv()
    mixed = red_c[0] + red_c[1]
    for axis in range(3):
        red_t[axis, pos[axis]] = mixed
        ref = red_t.at[axis, pos[axis]]
        copies = []
        for k, off in enumerate(OFFSETS):
            n = 1 + axis * 3 + k
            copies.append(put(ref, ref, red_send.at[n], red_recv.at[n], shifted(axis, off)))
        for copy in copies:
            copy.wait_recv()
        mixed = (red_t[axis, 0] + red_t[axis, 1]) + (red_t[axis, 2] + red_t[axis, 3])
    mixed = mixed * (1.0 / N)

    jj, cj, jc = mixed[:, 0:16], mixed[:, 16:32], mixed[:, 32:48]
    cc, cv = mixed[:, 48:64], mixed[:, 80:96]
    proj = cj + nt(cv, pc, HIGHEST)
    proj_ref[...] = proj
    a_cj = tn(proj, cj, HIGHEST)
    a_cc = tn(proj, cc, HIGHEST)
    gram = jj - a_cj - nn(jc - a_cc, proj, HIGHEST)

    eye = (lane_id[:, 0:16] == row_id[:, 0:16]).astype(F32)
    m = jnp.concatenate([gram, eye, jnp.zeros((16, 96), F32)], axis=1)
    for k in range(16):
        pivot_row = jnp.broadcast_to(m[k : k + 1, :], (16, 128))
        pivot = m[k : k + 1, k : k + 1]
        factor = jnp.broadcast_to(m[:, k : k + 1] / pivot, (16, 128))
        m = m - jnp.where(row_id > k, factor, 0.0) * pivot_row
    d = jnp.sum(jnp.where(lane_id == row_id, m, 0.0), axis=1, keepdims=True)
    m = m / jnp.sqrt(d)
    upper = jnp.where(lane_id[:, 0:16] >= row_id[:, 0:16], m[:, 0:16], 0.0)
    tri_ref[...] = upper.T
    inverse = m[:, 16:32]
    m2 = -nt(inverse, proj, HIGHEST)
    m1_hi, m1_lo = split(inverse)
    m2_hi, m2_lo = split(m2)
    lhs = jnp.concatenate(
        [
            jnp.concatenate([m1_hi, m1_hi, m2_hi, m2_hi], axis=1),
            jnp.concatenate([m1_lo, m1_lo, m2_lo, m2_lo], axis=1),
        ],
        axis=0,
    )

    def out_step(c, _):
        cols = pl.ds(pl.multiple_of(c * 1024, 1024), 1024)
        both = nn(lhs, stack[0:64, cols])
        out_ref[:, cols] = both[0:16] + both[16:32]
        return 0

    lax.fori_loop(0, ROWS // 1024, out_step, 0)
    for copy in sends:
        copy.wait_send()


def per_device(
    current, previous, prev_coupling, mass_diag, near_blocks, near_cols,
    cluster_basis, coupling, send_list, far_slot,
):
    dma = pltpu.SemaphoreType.DMA
    vmem = pl.BlockSpec(memory_space=pltpu.VMEM)
    hbm = pl.BlockSpec(memory_space=pl.ANY)
    return pl.pallas_call(
        kernel,
        out_shape=(
            jax.ShapeDtypeStruct((NRHS, ROWS), F32),
            jax.ShapeDtypeStruct((NRHS, NRHS), F32),
            jax.ShapeDtypeStruct((NRHS, NRHS), F32),
        ),
        in_specs=[hbm, hbm, vmem, hbm, hbm, vmem, hbm, hbm, vmem, vmem],
        out_specs=(vmem, vmem, vmem),
        scratch_shapes=[
            pltpu.VMEM((NRHS, ROWS), F32),
            pltpu.VMEM((NRHS, ROWS), F32),
            pltpu.VMEM((CPD, CL), F32),
            pltpu.VMEM((CPD * NNEAR, CL, CL), BF),
            pltpu.VMEM((CPD * RANK, CL), BF),
            pltpu.VMEM((CPD * RANK, NFAR * RANK), BF),
            pltpu.VMEM((3 * CPD, NRHS, CL), BF),
            pltpu.VMEM((96, ROWS), BF),
            pltpu.VMEM((NRHS, ROWS), F32),
            pltpu.VMEM((2, 4, 4, 4, PART_ROWS[0], 128), BF),
            pltpu.VMEM((2, 4, 4, 4, PART_ROWS[1], 128), BF),
            pltpu.VMEM((2, 4, 4, 4, PART_ROWS[2], 128), BF),
            pltpu.VMEM((128 * 18, 8, 128), F32),
            pltpu.VMEM((NFAR * RANK, 128), BF),
            pltpu.VMEM((8, 128), jnp.int32),
            pltpu.VMEM((NFAR, 128), jnp.int32),
            pltpu.VMEM((16, 128), jnp.int32),
            pltpu.SMEM((8, 128), jnp.int32),
            pltpu.SMEM((NFAR, 128), jnp.int32),
            pltpu.SMEM((16, 128), jnp.int32),
            pltpu.VMEM((2, 16, 128), F32),
            pltpu.VMEM((3, 4, 16, 128), F32),
            dma((5,)),
            dma((NEAR_CHUNKS,)),
            dma((3,)),
            dma((27,)),
            dma((27,)),
            dma((12,)),
            dma((12,)),
            dma((2,)),
            dma((2,)),
            dma((10,)),
            dma((10,)),
        ],
        compiler_params=pltpu.CompilerParams(
            collective_id=0, has_side_effects=True, vmem_limit_bytes=56 << 20
        ),
    )(
        current,
        previous,
        prev_coupling,
        mass_diag.reshape(CPD, CL),
        near_blocks.reshape(CPD * NNEAR, CL, CL),
        near_cols.T,
        cluster_basis.reshape(CPD * RANK, CL),
        coupling.reshape(CPD * RANK, NFAR * RANK),
        send_list[0].T,
        far_slot.T,
    )


def solution(mesh):
    placed = (
        P(None, ("group", "sub")),
        P(None, ("group", "sub")),
        P(),
        P(("group", "sub")),
        P(("group", "sub"), None, None, None),
        P(("group", "sub"), None),
        P(("group", "sub"), None, None),
        P(("group", "sub"), None, None),
        P(("group", "sub"), None, None),
        P(("group", "sub"), None),
    )
    return jax.shard_map(
        per_device,
        mesh=mesh,
        in_specs=placed,
        out_specs=(P(None, ("group", "sub")), P(), P()),
        check_vma=False,
    )
```

time: 263 us -> 82.1 us (0.31)
  blocking collectives: 125 us -> 0 us
  Pallas kernels: 0 us -> 75.4 us
  waiting for transfers between devices: 37.1 us -> 0 us
  matrix products: 34.9 us -> 0 us
  local copies, waits for them, and re-layouts: 35.7 us -> 5.65 us
  starting transfers between devices: 18.7 us -> 0 us
  other arithmetic: 9.61 us -> 0 us
    psum x2 -> x0, blocking collectives: 125 us -> none  [the longest x1 62.8 us: per_device(): lax.psum(jnp.dot(current, image.T, precision=highest), ('group', 'sub'))]
    pallas_call x0 -> x1, Pallas kernels: none -> 75.4 us  [per_device(): pl.pallas_call(kernel, out_shape=(jax.ShapeDtypeStruct((NRHS, ROWS), F32)...]
    ppermute x2 -> x0, waiting for transfers between devices: 37.1 us -> none  [the longest x1 31.3 us: with_halo(): after = lax.ppermute(leading, axis, down)]
    dot_general x8 -> x0, matrix products: 33.6 us -> none  [the longest x1 21.1 us: per_device(): jnp.einsum('rkm,rms->rks', coupling.astype(jnp.float32), picked, precisio...]
    gather x4 -> x0, local copies, waits for them, and re-layouts: 18 us -> none  [the longest x2 8.5 us: pack_slots(): chosen = coefficients[jnp.maximum(slot_ids, 0)]]
    reshape x3 -> x0, local copies, waits for them, and re-layouts: 16.1 us -> none  [the longest x1 12 us: per_device(): picked = picked.reshape(clusters, NFAR * RANK, rhs_count)]
    all_to_all x1 -> x0, starting transfers between devices: 11.6 us -> none  [per_device(): lax.all_to_all(packed, ('group', 'sub'), split_axis=0, concat_axis=0, til...]
    ppermute x2 -> x0, starting transfers between devices: 7.06 us -> none  [the longest x1 7.06 us: with_halo(): after = lax.ppermute(leading, axis, down)]
  transfers between devices with their start and end apart: 3 -> 0, of which waited for: 2 -> 0; matrix products, arithmetic and copies ran while one was open for 1% -> 0% of each run, Pallas kernels for 0% -> 0%
where the time goes in v1:
time: 82.1 us; the launch traced here: 81.7 us
  Pallas kernels  75.4 us (92%)
  local copies, waits for them, and re-layouts  5.65 us (7%)
    pallas_call x1, Pallas kernels, per_device(): pl.pallas_call(kernel, out_shape=(jax.ShapeDtypeStruct((NRHS, ROWS), F32)...  75.4 us
    unnamed x4, local copies, waits for them, and re-layouts  5.65 us

profile of v1, /device:TPU:0, one launch (start us, length us, event | category | flops | bytes accessed | tf_op | source)
XLA Modules:
  0.0 81.7 jit_solution(10166756587958292115)
XLA Ops:
  0.6 1.3 %copy.15 = s32[1,128,12]{1,2,0:T(8,128)} copy(s32[1,128,12]{1,0,2:T(1,128)} %param.18) | data formatting | bytes 12288
  1.9 75.4 %shard_map.121 = (f32[16,6144]{1,0:T(8,128)}, f32[16,16]{1,0:T(8,128)}, f32[16,16]{1,0:T(8,128)}) custom-call(f32[16,6144]{1,0:T(8,128)} %cur_h.1, f32[16,6144]{1,0:T(8,128)} %prev_h.1, f32[16,16]{1,0:T(8,128)} %pc_ref.1, f32[48,128]{1,0:T(8,128)} %bitcast.15, bf16[384,128,128]{2,1,0:T(8,128)(2,1)} %bitcast.11, s32[8,48]{1,0:T(8,128)} %bitcast.17, ...), custom_call_target="tpu_custom_call" | custom-call | tf_op jit(solution)/shard_map/pallas_call | solution.py:389
  77.4 1.8 %copy.19 = f32[16,6144]{1,0:T(8,128)} copy(f32[16,6144]{1,0:T(8,128)} %get-tuple-element.6) | data formatting | bytes 786432
  79.1 1.3 %copy.20 = f32[16,16]{1,0:T(8,128)} copy(f32[16,16]{1,0:T(8,128)} %get-tuple-element.7) | data formatting | bytes 2048
  80.4 1.3 %copy.21 = f32[16,16]{1,0:T(8,128)} copy(f32[16,16]{1,0:T(8,128)} %get-tuple-element.8) | data formatting | bytes 2048

commit v2 on v1

--- a/solution.py
+++ b/solution.py
@@ -22,7 +22,9 @@
 ROWS = CPD * CL
 NGRP = CPD // 8
 HIGHEST = lax.Precision.HIGHEST
-PART_ROWS = (64, 64, 32)
+PART_TILES = (4, 4, 3)
+PART_BASE = (0, 512, 1024)
+PER_TILE = 5
 ORDERS = ((0, 1, 2), (2, 0, 1), (1, 2, 0))
 OFFSETS = (2, 1, 3)
 NEAR_CHUNKS = 6
@@ -53,9 +55,9 @@
 
 def kernel(
     cur_h, prev_h, pc_ref, mass_h, near_h, ncol_ref, basis_h, coup_h, slist_ref, far_ref,
-    out_ref, proj_ref, tri_ref,
+    stack, mixed_ref,
     cur_v, prev_v, mass_v, near_v, basis_v, coup_v,
-    win, stack, jbuf, parts_a, parts_b, parts_c, table, xbuf,
+    win, vstack, jbuf, gathered, xbuf,
     ncol_v, far_v, addr_v, ncol_s, far_s, addr_s,
     red_c, red_t,
     load_sem, near_sem, smem_sem,
@@ -128,34 +130,6 @@
         return 0
 
     lax.fori_loop(0, CPD, window_step, 0, unroll=4)
-    loads[1].wait()
-    diag = lax.broadcasted_iota(jnp.int32, (8 * RANK, 128), 0) // RANK == (
-        lax.broadcasted_iota(jnp.int32, (8 * RANK, 128), 1) // NRHS
-    )
-    coefs = []
-    for g in range(NGRP):
-        cl = win[CPD + 8 * g : CPD + 8 * g + 8].reshape(128, CL)
-        y = nt(basis_v[192 * g : 192 * g + 192, :], cl)
-        y = jnp.where(diag, y, 0.0).reshape(8, RANK, 128)
-        coefs.append(jnp.sum(y, axis=0))
-    coefs = jnp.concatenate(coefs, axis=0).astype(BF)
-    slist = jnp.concatenate([slist_ref[...].astype(F32), jnp.zeros((4, 128), F32)], axis=0)
-    slist = slist.astype(BF)
-    bufs = (parts_a, parts_b, parts_c)
-
-    def block(p, phase, off):
-        at = [pos[a] for a in ORDERS[p]]
-        at[phase] = (at[phase] + off) % 4
-        return bufs[p].at[(core, at[2], at[1], at[0])[: 4 - phase]]
-
-    own = [tuple(pos[a] for a in ORDERS[p]) for p in range(3)]
-    i1, i2, i3 = own[0]
-    parts_a[core, i3, i2, i1] = coefs[0:64]
-    i1, i2, i3 = own[1]
-    parts_b[core, i3, i2, i1] = coefs[64:128]
-    i1, i2, i3 = own[2]
-    parts_c[core, i3, i2, i1] = jnp.concatenate([coefs[128:144], slist], axis=0)
-
     pl.semaphore_wait(barrier, len(peers))
 
     sends = []
@@ -168,6 +142,46 @@
         copy.start()
         sends.append(copy)
         return copy
+
+    mid = win.at[pl.ds(CPD, CPD)]
+    halo = [
+        put(mid, win.at[pl.ds(0, CPD)], halo_send.at[0], halo_recv.at[0], neighbour(1)),
+        put(mid, win.at[pl.ds(2 * CPD, CPD)], halo_send.at[1], halo_recv.at[1], neighbour(127)),
+    ]
+
+    loads[1].wait()
+    tiles = []
+    for m in range(10):
+        count = min(PER_TILE, CPD - m * PER_TILE)
+        cl = win[CPD + m * PER_TILE : CPD + m * PER_TILE + count].reshape(count * NRHS, CL)
+        y = nt(cl, basis_v[m * PER_TILE * RANK : (m * PER_TILE + count) * RANK, :])
+        shape = (count * NRHS, count * RANK)
+        diag = lax.broadcasted_iota(jnp.int32, shape, 0) // NRHS == (
+            lax.broadcasted_iota(jnp.int32, shape, 1) // RANK
+        )
+        y = jnp.sum(jnp.where(diag, y, 0.0).reshape(count, NRHS, count * RANK), axis=0)
+        y = jnp.concatenate([y, jnp.zeros((NRHS, 128 - count * RANK), F32)], axis=1)
+        tiles.append(y.astype(BF))
+    slist = jnp.concatenate([slist_ref[...].reshape(CAP, 128).astype(F32), jnp.zeros((4, 128), F32)], axis=0)
+    tiles.append(slist.astype(BF))
+
+    def block(p, phase, off):
+        at = [pos[a] for a in ORDERS[p]]
+        at[phase] = (at[phase] + off) % 4
+        size = PART_TILES[p]
+        first = ((core * 4 + at[2]) * 4 + at[1]) * 4 + at[0]
+        if phase == 1:
+            first, size = (core * 4 + at[2]) * 4 + at[1], size * 4
+        elif phase == 2:
+            first, size = core * 4 + at[2], size * 16
+        return gathered.at[pl.ds(PART_BASE[p] + first * size, size)]
+
+    done = 0
+    for p in range(3):
+        own = block(p, 0, 0)
+        for i in range(PART_TILES[p]):
+            own[i] = tiles[done + i]
+        done += PART_TILES[p]
 
     def gather_phase(phase):
         copies = []
@@ -187,11 +201,6 @@
         sib_copies.append(put(ref, ref, sib_send.at[n], sib_recv.at[n], sibling))
 
     phase1 = gather_phase(0)
-    mid = win.at[pl.ds(CPD, CPD)]
-    halo = [
-        put(mid, win.at[pl.ds(0, CPD)], halo_send.at[0], halo_recv.at[0], neighbour(1)),
-        put(mid, win.at[pl.ds(2 * CPD, CPD)], halo_send.at[1], halo_recv.at[1], neighbour(127)),
-    ]
     loads[2].wait()
     pc = pc_ref[...]
     pc_hi, pc_lo = split(pc)
@@ -202,8 +211,8 @@
     def previous_step(c, _):
         cols = pl.ds(pl.multiple_of(c * 512, 512), 512)
         hi, lo = split(prev_v[:, cols])
-        stack[64:80, cols] = hi
-        stack[80:96, cols] = lo
+        vstack[0:16, cols] = hi
+        vstack[16:32, cols] = lo
         both = nn(pc_all, jnp.concatenate([hi, lo], axis=0))
         jbuf[:, cols] = -(both[0:16] + both[16:32])
         return 0
@@ -251,53 +260,46 @@
     for copy in sib_copies:
         copy.wait_recv()
 
-    def table_step(t, _):
-        c, x, z, y = t // 64, t // 16 % 4, t // 4 % 4, t % 4
-        table[pl.ds(t * 18, 8)] = parts_a[c, z, y, x].astype(F32).reshape(8, 8, 128)
-        table[pl.ds(t * 18 + 8, 8)] = parts_b[c, y, x, z].astype(F32).reshape(8, 8, 128)
-        table[pl.ds(t * 18 + 16, 2)] = parts_c[c, x, z, y, 0:16].astype(F32).reshape(2, 8, 128)
-        return 0
-
-    lax.fori_loop(0, 128, table_step, 0)
-
-    lists = parts_c[:, :, :, :, 16:32].reshape(128 * 16, 128)
+    lists = gathered[PART_BASE[2] : PART_BASE[2] + 384].reshape(128, 3, 16, 128)[:, 2]
     mine = (lax.broadcasted_iota(jnp.int32, (16, 128), 1) == me).astype(BF)
-    local = nt(mine, lists)
-    row_id = lax.broadcasted_iota(jnp.int32, (16, 128), 0)
-    lane_id = lax.broadcasted_iota(jnp.int32, (16, 128), 1)
-    picked = jnp.zeros((16, 128), F32)
-    for i in range(16):
-        picked = jnp.where(row_id == i, local[:, i * 128 : (i + 1) * 128], picked)
-    picked = jnp.clip(picked.astype(jnp.int32), 0, CPD - 1)
-    first = (row_id * 8 + (lane_id >> 4)) * 18 + (picked >> 3) * 3
-    addr_v[...] = jnp.clip(first * 8 + (picked & 7), 0, (128 * 18 - 3) * 8 + 7)
+    local = nt(mine, lists.reshape(2048, 128))[0:1]
+    local = jnp.clip(local.astype(jnp.int32), 0, CPD - 1)
+    t = lax.broadcasted_iota(jnp.int32, (1, 2048), 1) >> 4
+    sy, sz, sx, sc = t & 3, (t >> 2) & 3, (t >> 4) & 3, t >> 6
+    tile = (local * 13) >> 6
+    at_a = (((sc * 4 + sz) * 4 + sy) * 4 + sx) * 4 + tile
+    at_b = PART_BASE[1] + (((sc * 4 + sy) * 4 + sx) * 4 + sz) * 4 + tile - 4
+    at_c = PART_BASE[2] + t * 3 + tile - 8
+    at = jnp.where(tile < 4, at_a, jnp.where(tile < 8, at_b, at_c))
+    turn = (128 - (local - tile * PER_TILE) * RANK) & 127
+    addr_v[...] = jnp.clip(at, 0, 1407) * 128 + turn
     addr_copy = pltpu.make_async_copy(addr_v, addr_s, smem_sem.at[2])
     addr_copy.start()
     addr_copy.wait()
 
-    lane_block = lax.broadcasted_iota(jnp.int32, (RANK, 128), 1) // NRHS
+    lane = lax.broadcasted_iota(jnp.int32, (16, 128), 1)
+    diag = lax.broadcasted_iota(jnp.int32, (128, 8 * RANK), 0) // NRHS == (
+        lax.broadcasted_iota(jnp.int32, (128, 8 * RANK), 1) // RANK
+    )
 
     def far_step(g, _):
-        def pick_step(jj, _):
-            halves = []
-            for k in range(2):
-                total = None
-                for r in range(8):
-                    at = far_s[jj * 2 + k, g * 8 + r]
-                    word = addr_s[at >> 7, at & 127]
-                    rows = table[pl.ds(word >> 3, 3)].reshape(RANK, 128)
-                    rows = pltpu.roll(rows, ((r - word) & 7) * NRHS, 1)
-                    total = rows if r == 0 else jnp.where(lane_block == r, rows, total)
-                halves.append(total)
-            both = jnp.concatenate(halves, axis=0).astype(BF)
-            xbuf[pl.ds(pl.multiple_of(jj * 48, 48), 48), :] = both
+        def pick_step(r, _):
+            total = [None] * 6
+            for j in range(NFAR):
+                word = addr_s[0, far_s[j, g * 8 + r]]
+                rows = pltpu.roll(gathered[word >> 7], (word + j * RANK) & 127, 1)
+                k, first = j * RANK // 128, j * RANK % 128
+                total[k] = rows if first == 0 else jnp.where(lane >= first, rows, total[k])
+                if first + RANK > 128:
+                    total[k + 1] = rows
+            xbuf[pl.ds(pl.multiple_of(r * 16, 16), 16), :] = jnp.concatenate(total, axis=1)
             return 0
 
-        lax.fori_loop(0, NFAR // 2, pick_step, 0)
+        lax.fori_loop(0, 8, pick_step, 0)
         rows = pl.ds(pl.multiple_of(g * 192, 192), 192)
-        combined = nn(coup_v[rows, :], xbuf[...])
+        combined = nt(xbuf[...], coup_v[rows, :])
         combined = jnp.where(diag, combined, 0.0).astype(BF)
-        far = tn(combined, basis_v[rows, :])
+        far = nn(combined, basis_v[rows, :])
         for r in range(8):
             cols = pl.ds(pl.multiple_of((g * 8 + r) * CL, CL), CL)
             val = jbuf[:, cols] + far[r * 16 : r * 16 + 16]
@@ -311,14 +313,14 @@
     def inner_step(c, total):
         cols = pl.ds(pl.multiple_of(c * 1024, 1024), 1024)
         s = stack[:, cols]
-        return total + nt(s[0:64], s)
+        return total + nt(s, jnp.concatenate([s, vstack[:, cols]], axis=0))
 
     inner = lax.fori_loop(0, ROWS // 1024, inner_step, jnp.zeros((64, 96), F32))
     inner = jnp.concatenate([inner, jnp.zeros((64, 32), F32)], axis=1)
     inner = inner + pltpu.roll(inner, 112, 1)
     j_rows = inner[0:16] + inner[16:32]
     c_rows = pltpu.roll(inner[32:48] + inner[48:64], 16, 1)
-    odd = (lane_id // 16) % 2 == 1
+    odd = (lane // 16) % 2 == 1
     mixed = jnp.where(odd, c_rows, j_rows)
 
     red_c[core] = mixed
@@ -335,8 +337,16 @@
         for copy in copies:
             copy.wait_recv()
         mixed = (red_t[axis, 0] + red_t[axis, 1]) + (red_t[axis, 2] + red_t[axis, 3])
-    mixed = mixed * (1.0 / N)
-
+    mixed_ref[...] = mixed * (1.0 / N)
+    for copy in sends:
+        copy.wait_send()
+
+
+def finish(stack, mixed_ref, pc_ref, out_ref, proj_ref, tri_ref):
+    mixed = mixed_ref[...]
+    pc = pc_ref[...]
+    row_id = lax.broadcasted_iota(jnp.int32, (16, 128), 0)
+    lane_id = lax.broadcasted_iota(jnp.int32, (16, 128), 1)
     jj, cj, jc = mixed[:, 0:16], mixed[:, 16:32], mixed[:, 32:48]
     cc, cv = mixed[:, 48:64], mixed[:, 80:96]
     proj = cj + nt(cv, pc, HIGHEST)
@@ -370,13 +380,11 @@
 
     def out_step(c, _):
         cols = pl.ds(pl.multiple_of(c * 1024, 1024), 1024)
-        both = nn(lhs, stack[0:64, cols])
+        both = nn(lhs, stack[:, cols])
         out_ref[:, cols] = both[0:16] + both[16:32]
         return 0
 
     lax.fori_loop(0, ROWS // 1024, out_step, 0)
-    for copy in sends:
-        copy.wait_send()
 
 
 def per_device(
@@ -386,15 +394,14 @@
     dma = pltpu.SemaphoreType.DMA
     vmem = pl.BlockSpec(memory_space=pltpu.VMEM)
     hbm = pl.BlockSpec(memory_space=pl.ANY)
-    return pl.pallas_call(
+    stack, mixed = pl.pallas_call(
         kernel,
         out_shape=(
-            jax.ShapeDtypeStruct((NRHS, ROWS), F32),
-            jax.ShapeDtypeStruct((NRHS, NRHS), F32),
-            jax.ShapeDtypeStruct((NRHS, NRHS), F32),
+            jax.ShapeDtypeStruct((64, ROWS), BF),
+            jax.ShapeDtypeStruct((NRHS, 128), F32),
         ),
         in_specs=[hbm, hbm, vmem, hbm, hbm, vmem, hbm, hbm, vmem, vmem],
-        out_specs=(vmem, vmem, vmem),
+        out_specs=(vmem, vmem),
         scratch_shapes=[
             pltpu.VMEM((NRHS, ROWS), F32),
             pltpu.VMEM((NRHS, ROWS), F32),
@@ -403,19 +410,16 @@
             pltpu.VMEM((CPD * RANK, CL), BF),
             pltpu.VMEM((CPD * RANK, NFAR * RANK), BF),
             pltpu.VMEM((3 * CPD, NRHS, CL), BF),
-            pltpu.VMEM((96, ROWS), BF),
+            pltpu.VMEM((32, ROWS), BF),
             pltpu.VMEM((NRHS, ROWS), F32),
-            pltpu.VMEM((2, 4, 4, 4, PART_ROWS[0], 128), BF),
-            pltpu.VMEM((2, 4, 4, 4, PART_ROWS[1], 128), BF),
-            pltpu.VMEM((2, 4, 4, 4, PART_ROWS[2], 128), BF),
-            pltpu.VMEM((128 * 18, 8, 128), F32),
-            pltpu.VMEM((NFAR * RANK, 128), BF),
+            pltpu.VMEM((128 * 11, NRHS, 128), BF),
+            pltpu.VMEM((128, NFAR * RANK), BF),
             pltpu.VMEM((8, 128), jnp.int32),
             pltpu.VMEM((NFAR, 128), jnp.int32),
-            pltpu.VMEM((16, 128), jnp.int32),
+            pltpu.VMEM((1, 2048), jnp.int32),
             pltpu.SMEM((8, 128), jnp.int32),
             pltpu.SMEM((NFAR, 128), jnp.int32),
-            pltpu.SMEM((16, 128), jnp.int32),
+            pltpu.SMEM((1, 2048), jnp.int32),
             pltpu.VMEM((2, 16, 128), F32),
             pltpu.VMEM((3, 4, 16, 128), F32),
             dma((5,)),
@@ -442,9 +446,19 @@
         near_cols.T,
         cluster_basis.reshape(CPD * RANK, CL),
         coupling.reshape(CPD * RANK, NFAR * RANK),
-        send_list[0].T,
+        send_list.transpose(2, 0, 1),
         far_slot.T,
     )
+    return pl.pallas_call(
+        finish,
+        out_shape=(
+            jax.ShapeDtypeStruct((NRHS, ROWS), F32),
+            jax.ShapeDtypeStruct((NRHS, NRHS), F32),
+            jax.ShapeDtypeStruct((NRHS, NRHS), F32),
+        ),
+        in_specs=[vmem, vmem, vmem],
+        out_specs=(vmem, vmem, vmem),
+    )(stack, mixed, prev_coupling)
 
 
 def solution(mesh):

time: 82.1 us -> 68.3 us (0.83)
  Pallas kernels: 75.4 us -> 67.5 us
  local copies, waits for them, and re-layouts: 5.65 us -> 0 us
    pallas_call x1 -> x2, Pallas kernels: 75.4 us -> 67.5 us  [the longest x1 62.3 us: per_device(): pl.pallas_call(kernel, out_shape=(jax.ShapeDtypeStruct((64, ROWS), BF), j...]
    unnamed x4 -> x0, local copies, waits for them, and re-layouts: 5.65 us -> none
where the time goes in v2:
time: 68.3 us; the launch traced here: 68.1 us
  Pallas kernels  67.5 us (99%)
    pallas_call x1, Pallas kernels, per_device(): pl.pallas_call(kernel, out_shape=(jax.ShapeDtypeStruct((64, ROWS), BF), j...  62.3 us
    pallas_call x1, Pallas kernels, per_device(): pl.pallas_call(finish, out_shape=(jax.ShapeDtypeStruct((NRHS, ROWS), F32)...  5.22 us

profile of v2, /device:TPU:0, one launch (start us, length us, event | category | flops | bytes accessed | tf_op | source)
XLA Modules:
  0.0 68.1 jit_solution(10124025027026124892)
XLA Ops:
  0.6 62.3 %shard_map.121 = (bf16[64,6144]{1,0:T(8,128)(2,1)}, f32[16,128]{1,0:T(8,128)}) custom-call(f32[16,6144]{1,0:T(8,128)} %cur_h.1, f32[16,6144]{1,0:T(8,128)} %prev_h.1, f32[16,16]{1,0:T(8,128)} %pc_ref.3, f32[48,128]{1,0:T(8,128)} %bitcast.10, bf16[384,128,128]{2,1,0:T(8,128)(2,1)} %bitcast.7, s32[8,48]{1,0:T(8,128)} %bitcast.13, bf16[1152,128]{1,0:T(8,128)(2,1)} %bitcast.9, ...), custom_call_target="tpu_custom_call" | custom-call | tf_op jit(solution)/shard_map/pallas_call | solution.py:397
  62.9 5.2 %shard_map.122 = (f32[16,6144]{1,0:T(8,128)}, f32[16,16]{1,0:T(8,128)}, f32[16,16]{1,0:T(8,128)}) custom-call(bf16[64,6144]{1,0:T(8,128)(2,1)} %get-tuple-element.5.stack, f32[16,128]{1,0:T(8,128)} %get-tuple-element.6.mixed_ref, f32[16,16]{1,0:T(8,128)} %pc_ref.3), custom_call_target="tpu_custom_call" | custom-call | tf_op jit(solution)/shard_map/pallas_call | solution.py:452

commit v3 on v2

v3 whole, which is shorter than its diff:
```python
import functools

import jax
import jax.numpy as jnp
from jax import lax
from jax.experimental import pallas as pl
from jax.experimental.pallas import tpu as pltpu
from jax.sharding import PartitionSpec as P

MESH = pl.DeviceIdType.MESH
BF = jnp.bfloat16
F32 = jnp.float32
NRHS = 16
CL = 128
RANK = 24
NNEAR = 8
NFAR = 32
CAP = 12
CPD = 48
NCL = 6144
N = 786432
ROWS = CPD * CL
NGRP = CPD // 8
HIGHEST = lax.Precision.HIGHEST
PART_TILES = (4, 4, 2)
PART_BASE = (0, 512, 1024)
PER_TILE = 5
ORDERS = ((0, 1, 2), (2, 0, 1), (1, 2, 0))
OFFSETS = (2, 1, 3)
VIA_UP = (0, 1)
XC = [(dx, dc) for dx in range(4) for dc in range(2) if dx or dc]
YZ = [(dy, dz) for dy in range(4) for dz in range(4) if dy or dz]
TILES = 1280
NEAR_CHUNKS = 6


def nt(a, b, precision=None):
    return lax.dot_general(
        a, b, (((1,), (1,)), ((), ())), preferred_element_type=F32, precision=precision
    )


def tn(a, b, precision=None):
    return lax.dot_general(
        a, b, (((0,), (0,)), ((), ())), preferred_element_type=F32, precision=precision
    )


def nn(a, b, precision=None):
    return lax.dot_general(
        a, b, (((1,), (0,)), ((), ())), preferred_element_type=F32, precision=precision
    )


def split(x):
    hi = x.astype(BF)
    return hi, (x - hi.astype(F32)).astype(BF)


def kernel(
    cur_h, prev_h, pc_h, mass_h, near_h, ncol_h, basis_h, coup_h, slist_h, far_h,
    stack_h, mixed_ref,
    cur_v, prev_v, pc_v, mass_v, near_v, basis_v, coup_v, slist_v, ncol_v, far_v,
    win, stack, vbuf, ibuf, gathered, lists, xbuf,
    addr_v, ncol_s, far_s, addr_s,
    red_a, red_b,
    load_sem, near_sem, smem_sem, out_sem,
    p1_send, p1_recv, p2_send, p2_recv, p3_send, p3_recv, list_send, list_recv,
    sib_send, sib_recv, halo_send, halo_recv, red_send, red_recv,
):
    grp = lax.axis_index("group")
    sub = lax.axis_index("sub")
    me = grp * 16 + sub
    core = grp % 2
    pos = (sub % 4, grp // 2, sub // 4)

    def place(x, y, z, c):
        return (y * 2 + c, z * 4 + x)

    def shifted(axis, off):
        at = list(pos)
        at[axis] = (at[axis] + off) % 4
        return place(*at, core)

    def at_xc(dx, dc):
        return place((pos[0] + dx) % 4, pos[1], pos[2], (core + dc) % 2)

    def at_yz(dy, dz):
        return place(pos[0], (pos[1] + dy) % 4, (pos[2] + dz) % 4, core)

    sibling = place(*pos, 1 - core)

    def neighbour(off):
        d = (me + off) % 128
        return (d // 16, d % 16)

    loads = {}
    for n, (name, src, dst) in enumerate(
        (
            ("cur", cur_h, cur_v), ("basis", basis_h, basis_v), ("slist", slist_h, slist_v),
            ("ncol", ncol_h, ncol_v), ("far", far_h, far_v), ("pc", pc_h, pc_v),
            ("prev", prev_h, prev_v), ("mass", mass_h, mass_v), ("coup", coup_h, coup_v),
        )
    ):
        loads[name] = pltpu.make_async_copy(src, dst, load_sem.at[n])
        loads[name].start()
    per = CPD * NNEAR // NEAR_CHUNKS
    near_loads = []
    for n in range(NEAR_CHUNKS):
        part = pl.ds(n * per, per)
        copy = pltpu.make_async_copy(near_h.at[part], near_v.at[part], near_sem.at[n])
        copy.start()
        near_loads.append(copy)

    peers = [at_xc(dx, dc) for dx, dc in XC] + [at_yz(dy, dz) for dy, dz in YZ]
    peers += [neighbour(1), neighbour(127)]
    barrier = pltpu.get_barrier_semaphore()
    for d in peers:
        pl.semaphore_signal(barrier, inc=1, device_id=d, device_id_type=MESH)

    loads["cur"].wait()

    def window_step(c, _):
        cols = pl.ds(pl.multiple_of(c * CL, CL), CL)
        hi, lo = split(cur_v[:, cols])
        win[CPD + c] = hi
        stack[32:48, cols] = hi
        stack[48:64, cols] = lo
        return 0

    lax.fori_loop(0, CPD, window_step, 0, unroll=4)
    pl.semaphore_wait(barrier, len(peers))

    sends = []

    def put(src_ref, dst_ref, send_sem, recv_sem, device):
        copy = pltpu.make_async_remote_copy(
            src_ref=src_ref, dst_ref=dst_ref, send_sem=send_sem, recv_sem=recv_sem,
            device_id=device, device_id_type=MESH,
        )
        copy.start()
        sends.append(copy)
        return copy

    mid = win.at[pl.ds(CPD, CPD)]
    halo = [
        put(mid, win.at[pl.ds(0, CPD)], halo_send.at[0], halo_recv.at[0], neighbour(1)),
        put(mid, win.at[pl.ds(2 * CPD, CPD)], halo_send.at[1], halo_recv.at[1], neighbour(127)),
    ]

    loads["basis"].wait()
    tiles = []
    for m in range(10):
        count = min(PER_TILE, CPD - m * PER_TILE)
        cl = win[CPD + m * PER_TILE : CPD + m * PER_TILE + count].reshape(count * NRHS, CL)
        y = nt(cl, basis_v[m * PER_TILE * RANK : (m * PER_TILE + count) * RANK, :])
        shape = (count * NRHS, count * RANK)
        diag = lax.broadcasted_iota(jnp.int32, shape, 0) // NRHS == (
            lax.broadcasted_iota(jnp.int32, shape, 1) // RANK
        )
        y = jnp.sum(jnp.where(diag, y, 0.0).reshape(count, NRHS, count * RANK), axis=0)
        y = jnp.concatenate([y, jnp.zeros((NRHS, 128 - count * RANK), F32)], axis=1)
        tiles.append(y.astype(BF))
    loads["slist"].wait()
    slist = slist_v[...].reshape(CAP, 128).astype(F32)
    slist = jnp.concatenate([slist, jnp.zeros((4, 128), F32)], axis=0).astype(BF)

    def chunk(p):
        at = [pos[a] for a in ORDERS[p]]
        first = ((core * 4 + at[2]) * 4 + at[1]) * 4 + at[0]
        return gathered.at[pl.ds(PART_BASE[p] + first * PART_TILES[p], PART_TILES[p])]

    def rows_of(p, k2, k3):
        at = [pos[a] for a in ORDERS[p]]
        first = (core * 4 + (at[2] + k3) % 4) * 4 + (at[1] + k2) % 4
        size = 4 * PART_TILES[p]
        return gathered.at[pl.ds(PART_BASE[p] + first * size, size)]

    def plane_of(p):
        size = 16 * PART_TILES[p]
        return gathered.at[pl.ds(PART_BASE[p] + (core * 4 + pos[ORDERS[p][2]]) * size, size)]

    def list_block(phase):
        first = core * 64 + pos[2] * 16
        if phase < 2:
            first = first + pos[1] * 4
        if phase < 1:
            first = first + pos[0]
        return lists.at[pl.ds(first, 4**phase)]

    done = 0
    for p in range(3):
        own = chunk(p)
        for i in range(PART_TILES[p]):
            own[i] = tiles[done + i]
        done += PART_TILES[p]
    list_block(0)[0] = slist

    def spread(ref, axis, sems, n):
        return {
            off: put(ref, ref, sems[0].at[n + k], sems[1].at[n + k], shifted(axis, off))
            for k, off in enumerate(OFFSETS)
        }

    def spread_list(phase):
        return spread(list_block(phase), phase, (list_send, list_recv), 3 * phase)

    def arrive(copies):
        for copy in copies.values():
            copy.wait_recv()

    sib_copies = []

    def to_sibling(ref):
        n = len(sib_copies)
        sib_copies.append(put(ref, ref, sib_send.at[n], sib_recv.at[n], sibling))

    phase3 = {}

    def start3(p, k2):
        axis = ORDERS[p][2]
        ref = rows_of(p, k2, 0)
        n = (p * 4 + k2) * 3
        phase3[p, k2] = [
            put(ref, ref, p3_send.at[n], p3_recv.at[n], shifted(axis, 1)),
            put(ref, ref, p3_send.at[n + 1], p3_recv.at[n + 1], shifted(axis, 3)),
        ]

    def relay3(k2):
        for p in range(3):
            axis = ORDERS[p][2]
            n = (p * 4 + k2) * 3 + 2
            up = k2 in VIA_UP
            phase3[p, k2][0 if up else 1].wait_recv()
            ref = rows_of(p, k2, 3 if up else 1)
            phase3[p, k2].append(
                put(ref, ref, p3_send.at[n], p3_recv.at[n], shifted(axis, 1 if up else 3))
            )
        for p in range(3):
            phase3[p, k2][1 if k2 in VIA_UP else 0].wait_recv()

    phase1 = [spread(chunk(p), ORDERS[p][0], (p1_send, p1_recv), 3 * p) for p in range(3)]
    lists1 = spread_list(0)

    loads["ncol"].wait()
    wanted = ncol_v[...] - (me - 1) * CPD
    wanted = jnp.where(wanted < 0, wanted + NCL, wanted)
    wanted = jnp.where(wanted >= NCL, wanted - NCL, wanted)
    ncol_v[...] = jnp.clip(wanted, 0, 3 * CPD - 1)
    loads["far"].wait()
    q = far_v[...]
    src = (q * 43691) >> 19
    slot = q - src * CAP
    src_g, src_s = src >> 4, src & 15
    order = (src_g & 1) * 64 + (src_s >> 2) * 16 + (src_g >> 1) * 4 + (src_s & 3)
    far_v[...] = jnp.clip(order * 16 + slot, 0, 2047)
    ncol_copy = pltpu.make_async_copy(ncol_v, ncol_s, smem_sem.at[0])
    far_copy = pltpu.make_async_copy(far_v, far_s, smem_sem.at[1])
    ncol_copy.start()
    far_copy.start()

    loads["pc"].wait()
    loads["prev"].wait()
    pc = pc_v[...]
    pc_hi, pc_lo = split(pc)
    pc_rows = jnp.concatenate([pc_hi, pc_hi], axis=1)
    pc_rows2 = jnp.concatenate([pc_lo, pc_lo], axis=1)
    pc_all = jnp.concatenate([pc_rows, pc_rows2], axis=0)

    def previous_step(c, _):
        cols = pl.ds(pl.multiple_of(c * 512, 512), 512)
        hi, lo = split(prev_v[:, cols])
        both = nn(pc_all, jnp.concatenate([hi, lo], axis=0))
        vbuf[:, cols] = both[0:16] + both[16:32]
        return 0

    lax.fori_loop(0, ROWS // 512, previous_step, 0)

    for copies in phase1:
        arrive(copies)
    arrive(lists1)
    lists2 = spread_list(1)
    phase2 = [spread(rows_of(p, 0, 0), ORDERS[p][1], (p2_send, p2_recv), 3 * p) for p in range(3)]
    for p in range(3):
        start3(p, 0)
    loads["mass"].wait()
    loads["coup"].wait()
    ncol_copy.wait()
    far_copy.wait()
    arrive(lists2)
    lists3 = spread_list(2)
    for k2, off in ((1, 3), (3, 1), (2, 2)):
        if k2 == 2:
            relay3(0)
        for p in range(3):
            phase2[p][off].wait_recv()
            start3(p, k2)
    for p in range(3):
        to_sibling(plane_of(p))

    for copy in halo:
        copy.wait_recv()

    def near_step(r, _):
        xs, ms = [], []
        for j in range(NNEAR):
            w = ncol_s[j, r]
            xs.append(win[w])
        x = jnp.concatenate(xs, axis=1)
        m = near_v[pl.ds(r * NNEAR, NNEAR)]
        m = jnp.concatenate([m[j] for j in range(NNEAR)], axis=1)
        cols = pl.ds(pl.multiple_of(r * CL, CL), CL)
        ibuf[:, cols] = nt(x, m) + mass_v[pl.ds(r, 1), :] * cur_v[:, cols]
        return 0

    def near_chunk(n):
        rows_per = CPD // NEAR_CHUNKS
        near_loads[n].wait()
        lax.fori_loop(n * rows_per, (n + 1) * rows_per, near_step, 0, unroll=4)

    def forward3(k2):
        for p in range(3):
            to_sibling(rows_of(p, k2, 1))
            to_sibling(rows_of(p, k2, 3))

    near_chunk(0)
    arrive(lists3)
    list_plane = lists.at[pl.ds(core * 64, 64)]
    list_sib = put(list_plane, list_plane, list_send.at[9], list_recv.at[9], sibling)
    near_chunk(1)
    relay3(1)
    forward3(0)
    forward3(1)
    near_chunk(2)
    near_chunk(3)
    relay3(3)
    forward3(3)
    near_chunk(4)
    list_sib.wait_recv()

    mine = (lax.broadcasted_iota(jnp.int32, (16, 128), 1) == me).astype(BF)
    local = nt(mine, lists[...].reshape(2048, 128))[0:1]
    local = jnp.clip(local.astype(jnp.int32), 0, CPD - 1)
    t = lax.broadcasted_iota(jnp.int32, (1, 2048), 1) >> 4
    sx, sy, sz, sc = t & 3, (t >> 2) & 3, (t >> 4) & 3, t >> 6
    tile = (local * 13) >> 6
    at_a = (((sc * 4 + sz) * 4 + sy) * 4 + sx) * 4 + tile
    at_b = PART_BASE[1] + (((sc * 4 + sy) * 4 + sx) * 4 + sz) * 4 + tile - 4
    at_c = PART_BASE[2] + (((sc * 4 + sx) * 4 + sz) * 4 + sy) * 2 + tile - 8
    at = jnp.where(tile < 4, at_a, jnp.where(tile < 8, at_b, at_c))
    turn = (128 - (local - tile * PER_TILE) * RANK) & 127
    addr_v[...] = jnp.clip(at, 0, TILES - 1) * 128 + turn
    addr_copy = pltpu.make_async_copy(addr_v, addr_s, smem_sem.at[2])
    addr_copy.start()
    near_chunk(5)
    relay3(2)
    forward3(2)
    for k2 in (0, 1, 3, 2):
        for p in range(3):
            phase3[p, k2][2].wait_recv()
            to_sibling(rows_of(p, k2, 2))
    addr_copy.wait()
    for copy in sib_copies:
        copy.wait_recv()

    lane = lax.broadcasted_iota(jnp.int32, (16, 128), 1)
    diag = lax.broadcasted_iota(jnp.int32, (128, 8 * RANK), 0) // NRHS == (
        lax.broadcasted_iota(jnp.int32, (128, 8 * RANK), 1) // RANK
    )

    def far_step(g, total_inner):
        def pick_step(r, _):
            total = [None] * 6
            for j in range(NFAR):
                word = addr_s[0, far_s[j, g * 8 + r]]
                rows = pltpu.roll(gathered[word >> 7], (word + j * RANK) & 127, 1)
                k, first = j * RANK // 128, j * RANK % 128
                total[k] = rows if first == 0 else jnp.where(lane >= first, rows, total[k])
                if first + RANK > 128:
                    total[k + 1] = rows
            xbuf[pl.ds(pl.multiple_of(r * 16, 16), 16), :] = jnp.concatenate(total, axis=1)
            return 0

        lax.fori_loop(0, 8, pick_step, 0, unroll=8)
        rows = pl.ds(pl.multiple_of(g * 192, 192), 192)
        combined = nt(xbuf[...], coup_v[rows, :])
        combined = jnp.where(diag, combined, 0.0).astype(BF)
        far = nn(combined, basis_v[rows, :])
        cols = pl.ds(pl.multiple_of(g * 1024, 1024), 1024)
        far = jnp.concatenate([far[r * 16 : r * 16 + 16] for r in range(8)], axis=1)
        image = ibuf[:, cols] + far
        j_hi, j_lo = split(image - vbuf[:, cols])
        i_hi, i_lo = split(image)
        stack[0:16, cols] = j_hi
        stack[16:32, cols] = j_lo
        s = jnp.concatenate([j_hi, j_lo, stack[32:64, cols]], axis=0)
        return total_inner + nt(s, jnp.concatenate([s, i_hi, i_lo], axis=0))

    inner = lax.fori_loop(0, NGRP, far_step, jnp.zeros((64, 96), F32))
    stack_copy = pltpu.make_async_copy(stack, stack_h, out_sem)
    stack_copy.start()

    inner = jnp.concatenate([inner, jnp.zeros((64, 32), F32)], axis=1)
    inner = inner + pltpu.roll(inner, 112, 1)
    j_rows = inner[0:16] + inner[16:32]
    c_rows = inner[32:48] + inner[48:64]
    mixed = jnp.where(lane < 48, c_rows, pltpu.roll(c_rows, 112, 1))
    mixed = jnp.where(lane < 32, pltpu.roll(c_rows, 16, 1), mixed)
    mixed = jnp.where(lane < 16, j_rows, mixed)
    mixed = jnp.where(lane[0:8] < 64, mixed[0:8], pltpu.roll(mixed[8:16], 64, 1))

    def reduce(value, buf, place_at, devices, n):
        buf[place_at] = value
        ref = buf.at[place_at]
        copies = [
            put(ref, ref, red_send.at[n + k], red_recv.at[n + k], d) for k, d in enumerate(devices)
        ]
        for copy in copies:
            copy.wait_recv()
        parts = [buf[k] for k in range(len(devices) + 1)]
        while len(parts) > 1:
            parts = [a + b for a, b in zip(parts[::2], parts[1::2])]
        return parts[0]

    mixed = reduce(mixed, red_a, pos[0] * 2 + core, [at_xc(*o) for o in XC], 0)
    mixed = reduce(mixed, red_b, pos[1] * 4 + pos[2], [at_yz(*o) for o in YZ], 7)
    mixed_ref[...] = mixed * (1.0 / N)
    stack_copy.wait()
    for copy in sends:
        copy.wait_send()


def finish(stack_h, mixed_ref, out_h, proj_ref, tri_ref, stack, out_v, load_sem, out_sem):
    half = ROWS // 2
    loads = []
    for n in range(2):
        part = pl.ds(n * half, half)
        loads.append(
            pltpu.make_async_copy(stack_h.at[:, part], stack.at[:, part], load_sem.at[n])
        )
        loads[n].start()
    mixed = mixed_ref[...]
    mixed = jnp.concatenate([mixed, pltpu.roll(mixed, 64, 1)], axis=0)
    row_id = lax.broadcasted_iota(jnp.int32, (16, 128), 0)
    lane_id = lax.broadcasted_iota(jnp.int32, (16, 128), 1)
    jj, cj, cc, proj = mixed[:, 0:16], mixed[:, 16:32], mixed[:, 32:48], mixed[:, 48:64]
    proj_ref[...] = proj
    both = tn(proj, mixed[:, 16:48], HIGHEST)
    gram = jj - both[:, 0:16] - nn(cj.T - both[:, 16:32], proj, HIGHEST)

    eye = (lane_id[:, 0:16] == row_id[:, 0:16]).astype(F32)
    m = jnp.concatenate([gram, eye, jnp.zeros((16, 96), F32)], axis=1)
    for k in range(16):
        pivot_row = jnp.broadcast_to(m[k : k + 1, :], (16, 128))
        pivot = m[k : k + 1, k : k + 1]
        factor = jnp.broadcast_to(m[:, k : k + 1] / pivot, (16, 128))
        m = m - jnp.where(row_id > k, factor, 0.0) * pivot_row
    d = jnp.sum(jnp.where(lane_id == row_id, m, 0.0), axis=1, keepdims=True)
    m = m / jnp.sqrt(d)
    upper = jnp.where(lane_id[:, 0:16] >= row_id[:, 0:16], m[:, 0:16], 0.0)
    tri_ref[...] = upper.T
    inverse = m[:, 16:32]
    m2 = -nt(inverse, proj, HIGHEST)
    m1_hi, m1_lo = split(inverse)
    m2_hi, m2_lo = split(m2)
    lhs = jnp.concatenate(
        [
            jnp.concatenate([m1_hi, m1_hi, m2_hi, m2_hi], axis=1),
            jnp.concatenate([m1_lo, m1_lo, m2_lo, m2_lo], axis=1),
        ],
        axis=0,
    )

    def out_step(c, _):
        cols = pl.ds(pl.multiple_of(c * 1024, 1024), 1024)
        both = nn(lhs, stack[:, cols])
        out_v[:, cols] = both[0:16] + both[16:32]
        return 0

    stores = []
    for n in range(2):
        part = pl.ds(n * half, half)
        loads[n].wait()
        lax.fori_loop(n * 3, n * 3 + 3, out_step, 0, unroll=3)
        stores.append(pltpu.make_async_copy(out_v.at[:, part], out_h.at[:, part], out_sem.at[n]))
        stores[n].start()
    for copy in stores:
        copy.wait()


def per_device(
    current, previous, prev_coupling, mass_diag, near_blocks, near_cols,
    cluster_basis, coupling, send_list, far_slot,
):
    dma = pltpu.SemaphoreType.DMA
    vmem = pl.BlockSpec(memory_space=pltpu.VMEM)
    hbm = pl.BlockSpec(memory_space=pl.ANY)
    stack, mixed = pl.pallas_call(
        kernel,
        out_shape=(
            jax.ShapeDtypeStruct((64, ROWS), BF),
            jax.ShapeDtypeStruct((8, 128), F32),
        ),
        in_specs=[hbm] * 10,
        out_specs=(hbm, vmem),
        scratch_shapes=[
            pltpu.VMEM((NRHS, ROWS), F32),
            pltpu.VMEM((NRHS, ROWS), F32),
            pltpu.VMEM((NRHS, NRHS), F32),
            pltpu.VMEM((CPD, CL), F32),
            pltpu.VMEM((CPD * NNEAR, CL, CL), BF),
            pltpu.VMEM((CPD * RANK, CL), BF),
            pltpu.VMEM((CPD * RANK, NFAR * RANK), BF),
            pltpu.VMEM((CAP, 1, 128), jnp.int32),
            pltpu.VMEM((NNEAR, CPD), jnp.int32),
            pltpu.VMEM((NFAR, CPD), jnp.int32),
            pltpu.VMEM((3 * CPD, NRHS, CL), BF),
            pltpu.VMEM((64, ROWS), BF),
            pltpu.VMEM((NRHS, ROWS), F32),
            pltpu.VMEM((NRHS, ROWS), F32),
            pltpu.VMEM((TILES, NRHS, 128), BF),
            pltpu.VMEM((128, NRHS, 128), BF),
            pltpu.VMEM((128, NFAR * RANK), BF),
            pltpu.VMEM((1, 2048), jnp.int32),
            pltpu.SMEM((NNEAR, CPD), jnp.int32),
            pltpu.SMEM((NFAR, CPD), jnp.int32),
            pltpu.SMEM((1, 2048), jnp.int32),
            pltpu.VMEM((8, 8, 128), F32),
            pltpu.VMEM((16, 8, 128), F32),
            dma((9,)),
            dma((NEAR_CHUNKS,)),
            dma((3,)),
            dma,
            dma((9,)),
            dma((9,)),
            dma((9,)),
            dma((9,)),
            dma((36,)),
            dma((36,)),
            dma((10,)),
            dma((10,)),
            dma((39,)),
            dma((39,)),
            dma((2,)),
            dma((2,)),
            dma((22,)),
            dma((22,)),
        ],
        compiler_params=pltpu.CompilerParams(
            collective_id=0, has_side_effects=True, vmem_limit_bytes=56 << 20
        ),
    )(
        current,
        previous,
        prev_coupling,
        mass_diag.reshape(CPD, CL),
        near_blocks.reshape(CPD * NNEAR, CL, CL),
        near_cols.T,
        cluster_basis.reshape(CPD * RANK, CL),
        coupling.reshape(CPD * RANK, NFAR * RANK),
        send_list.transpose(2, 0, 1),
        far_slot.T,
    )
    return pl.pallas_call(
        finish,
        out_shape=(
            jax.ShapeDtypeStruct((NRHS, ROWS), F32),
            jax.ShapeDtypeStruct((NRHS, NRHS), F32),
            jax.ShapeDtypeStruct((NRHS, NRHS), F32),
        ),
        in_specs=[hbm, vmem],
        out_specs=(hbm, vmem, vmem),
        scratch_shapes=[
            pltpu.VMEM((64, ROWS), BF),
            pltpu.VMEM((NRHS, ROWS), F32),
            dma((2,)),
            dma((2,)),
        ],
    )(stack, mixed)


def solution(mesh):
    placed = (
        P(None, ("group", "sub")),
        P(None, ("group", "sub")),
        P(),
        P(("group", "sub")),
        P(("group", "sub"), None, None, None),
        P(("group", "sub"), None),
        P(("group", "sub"), None, None),
        P(("group", "sub"), None, None),
        P(("group", "sub"), None, None),
        P(("group", "sub"), None),
    )
    return jax.shard_map(
        per_device,
        mesh=mesh,
        in_specs=placed,
        out_specs=(P(None, ("group", "sub")), P(), P()),
        check_vma=False,
    )
```

time: 68.3 us -> 57.9 us (0.85)
  Pallas kernels: 67.5 us -> 57.1 us
    pallas_call x1, Pallas kernels: 62.3 us -> 52.6 us  [per_device(): pl.pallas_call(kernel, out_shape=(jax.ShapeDtypeStruct((64, ROWS), BF), j...]
where the time goes in v3:
time: 57.9 us; the launch traced here: 57.8 us
  Pallas kernels  57.1 us (99%)
  between operations  0.64 us (1%)
    pallas_call x1, Pallas kernels, per_device(): pl.pallas_call(kernel, out_shape=(jax.ShapeDtypeStruct((64, ROWS), BF), j...  52.6 us
    pallas_call x1, Pallas kernels, per_device(): pl.pallas_call(finish, out_shape=(jax.ShapeDtypeStruct((NRHS, ROWS), F32)...  4.57 us

profile of v3, /device:TPU:0, one launch (start us, length us, event | category | flops | bytes accessed | tf_op | source)
XLA Modules:
  0.0 57.8 jit_solution(2370647840772740322)
XLA Ops:
  0.6 52.6 %shard_map.121 = (bf16[64,6144]{1,0:T(8,128)(2,1)}, f32[8,128]{1,0:T(8,128)}) custom-call(f32[16,6144]{1,0:T(8,128)} %cur_h.1, f32[16,6144]{1,0:T(8,128)} %prev_h.1, f32[16,16]{1,0:T(8,128)} %pc_h.1, f32[48,128]{1,0:T(8,128)} %bitcast.10, bf16[384,128,128]{2,1,0:T(8,128)(2,1)} %bitcast.7, s32[8,48]{1,0:T(8,128)} %bitcast.13, bf16[1152,128]{1,0:T(8,128)(2,1)} %bitcast.9, ...), custom_call_target="tpu_custom_call" | custom-call | tf_op jit(solution)/shard_map/pallas_call | solution.py:498
  53.2 4.6 %shard_map.122 = (f32[16,6144]{1,0:T(8,128)}, f32[16,16]{1,0:T(8,128)}, f32[16,16]{1,0:T(8,128)}) custom-call(bf16[64,6144]{1,0:T(8,128)(2,1)} %get-tuple-element.5.stack_h, f32[8,128]{1,0:T(8,128)} %get-tuple-element.6.mixed_ref), custom_call_target="tpu_custom_call" | custom-call | tf_op jit(solution)/shard_map/pallas_call | solution.py:564

commit v4 on v3

--- a/solution.py
+++ b/solution.py
@@ -27,10 +27,11 @@
 PER_TILE = 5
 ORDERS = ((0, 1, 2), (2, 0, 1), (1, 2, 0))
 OFFSETS = (2, 1, 3)
-VIA_UP = (0, 1)
+RELAY_UP, RELAY_DOWN = (0, 3), (1,)
 XC = [(dx, dc) for dx in range(4) for dc in range(2) if dx or dc]
 YZ = [(dy, dz) for dy in range(4) for dz in range(4) if dy or dz]
 TILES = 1280
+FAR_UNROLL = 6
 NEAR_CHUNKS = 6
 
 
@@ -142,12 +143,6 @@
         sends.append(copy)
         return copy
 
-    mid = win.at[pl.ds(CPD, CPD)]
-    halo = [
-        put(mid, win.at[pl.ds(0, CPD)], halo_send.at[0], halo_recv.at[0], neighbour(1)),
-        put(mid, win.at[pl.ds(2 * CPD, CPD)], halo_send.at[1], halo_recv.at[1], neighbour(127)),
-    ]
-
     loads["basis"].wait()
     tiles = []
     for m in range(10):
@@ -221,26 +216,37 @@
         axis = ORDERS[p][2]
         ref = rows_of(p, k2, 0)
         n = (p * 4 + k2) * 3
-        phase3[p, k2] = [
-            put(ref, ref, p3_send.at[n], p3_recv.at[n], shifted(axis, 1)),
-            put(ref, ref, p3_send.at[n + 1], p3_recv.at[n + 1], shifted(axis, 3)),
-        ]
+        phase3[p, k2] = copies = []
+        if k2 not in RELAY_UP + RELAY_DOWN:
+            copies.append(put(ref, ref, p3_send.at[n], p3_recv.at[n], shifted(axis, 2)))
+        copies.append(put(ref, ref, p3_send.at[n + 1], p3_recv.at[n + 1], shifted(axis, 1)))
+        copies.append(put(ref, ref, p3_send.at[n + 2], p3_recv.at[n + 2], shifted(axis, 3)))
 
     def relay3(k2):
+        if k2 not in RELAY_UP + RELAY_DOWN:
+            for p in range(3):
+                phase3[p, k2][1].wait_recv()
+                phase3[p, k2][2].wait_recv()
+            return
+        up = k2 in RELAY_UP
         for p in range(3):
             axis = ORDERS[p][2]
-            n = (p * 4 + k2) * 3 + 2
-            up = k2 in VIA_UP
+            n = (p * 4 + k2) * 3
             phase3[p, k2][0 if up else 1].wait_recv()
             ref = rows_of(p, k2, 3 if up else 1)
-            phase3[p, k2].append(
-                put(ref, ref, p3_send.at[n], p3_recv.at[n], shifted(axis, 1 if up else 3))
-            )
+            copy = put(ref, ref, p3_send.at[n], p3_recv.at[n], shifted(axis, 1 if up else 3))
+            phase3[p, k2].insert(0, copy)
         for p in range(3):
-            phase3[p, k2][1 if k2 in VIA_UP else 0].wait_recv()
+            phase3[p, k2][2 if up else 1].wait_recv()
 
     phase1 = [spread(chunk(p), ORDERS[p][0], (p1_send, p1_recv), 3 * p) for p in range(3)]
     lists1 = spread_list(0)
+
+    mid = win.at[pl.ds(CPD, CPD)]
+    halo = [
+        put(mid, win.at[pl.ds(0, CPD)], halo_send.at[0], halo_recv.at[0], neighbour(1)),
+        put(mid, win.at[pl.ds(2 * CPD, CPD)], halo_send.at[1], halo_recv.at[1], neighbour(127)),
+    ]
 
     loads["ncol"].wait()
     wanted = ncol_v[...] - (me - 1) * CPD
@@ -357,7 +363,7 @@
     forward3(2)
     for k2 in (0, 1, 3, 2):
         for p in range(3):
-            phase3[p, k2][2].wait_recv()
+            phase3[p, k2][0].wait_recv()
             to_sibling(rows_of(p, k2, 2))
     addr_copy.wait()
     for copy in sib_copies:
@@ -368,35 +374,35 @@
         lax.broadcasted_iota(jnp.int32, (128, 8 * RANK), 1) // RANK
     )
 
-    def far_step(g, total_inner):
-        def pick_step(r, _):
-            total = [None] * 6
-            for j in range(NFAR):
-                word = addr_s[0, far_s[j, g * 8 + r]]
-                rows = pltpu.roll(gathered[word >> 7], (word + j * RANK) & 127, 1)
-                k, first = j * RANK // 128, j * RANK % 128
-                total[k] = rows if first == 0 else jnp.where(lane >= first, rows, total[k])
-                if first + RANK > 128:
-                    total[k + 1] = rows
-            xbuf[pl.ds(pl.multiple_of(r * 16, 16), 16), :] = jnp.concatenate(total, axis=1)
-            return 0
-
-        lax.fori_loop(0, 8, pick_step, 0, unroll=8)
-        rows = pl.ds(pl.multiple_of(g * 192, 192), 192)
-        combined = nt(xbuf[...], coup_v[rows, :])
-        combined = jnp.where(diag, combined, 0.0).astype(BF)
-        far = nn(combined, basis_v[rows, :])
-        cols = pl.ds(pl.multiple_of(g * 1024, 1024), 1024)
-        far = jnp.concatenate([far[r * 16 : r * 16 + 16] for r in range(8)], axis=1)
-        image = ibuf[:, cols] + far
-        j_hi, j_lo = split(image - vbuf[:, cols])
-        i_hi, i_lo = split(image)
-        stack[0:16, cols] = j_hi
-        stack[16:32, cols] = j_lo
-        s = jnp.concatenate([j_hi, j_lo, stack[32:64, cols]], axis=0)
-        return total_inner + nt(s, jnp.concatenate([s, i_hi, i_lo], axis=0))
-
-    inner = lax.fori_loop(0, NGRP, far_step, jnp.zeros((64, 96), F32))
+    def far_step(i, total):
+        for u in range(FAR_UNROLL):
+            g = i * FAR_UNROLL + u
+            for r in range(8):
+                row = [None] * 6
+                for j in range(NFAR):
+                    word = addr_s[0, far_s[j, g * 8 + r]]
+                    tile = pltpu.roll(gathered[word >> 7], (word + j * RANK) & 127, 1)
+                    k, first = j * RANK // 128, j * RANK % 128
+                    row[k] = tile if first == 0 else jnp.where(lane >= first, tile, row[k])
+                    if first + RANK > 128:
+                        row[k + 1] = tile
+                xbuf[u, r * 16 : r * 16 + 16, :] = jnp.concatenate(row, axis=1)
+            rows = pl.ds(pl.multiple_of(g * 192, 192), 192)
+            combined = nt(xbuf[u], coup_v[rows, :])
+            combined = jnp.where(diag, combined, 0.0).astype(BF)
+            far = nn(combined, basis_v[rows, :])
+            cols = pl.ds(pl.multiple_of(g * 1024, 1024), 1024)
+            far = jnp.concatenate([far[r * 16 : r * 16 + 16] for r in range(8)], axis=1)
+            image = ibuf[:, cols] + far
+            j_hi, j_lo = split(image - vbuf[:, cols])
+            i_hi, i_lo = split(image)
+            stack[0:16, cols] = j_hi
+            stack[16:32, cols] = j_lo
+            s = jnp.concatenate([j_hi, j_lo, stack[32:64, cols]], axis=0)
+            total = total + nt(s, jnp.concatenate([s, i_hi, i_lo], axis=0))
+        return total
+
+    inner = lax.fori_loop(0, NGRP // FAR_UNROLL, far_step, jnp.zeros((64, 96), F32))
     stack_copy = pltpu.make_async_copy(stack, stack_h, out_sem)
     stack_copy.start()
 
@@ -520,7 +526,7 @@
             pltpu.VMEM((NRHS, ROWS), F32),
             pltpu.VMEM((TILES, NRHS, 128), BF),
             pltpu.VMEM((128, NRHS, 128), BF),
-            pltpu.VMEM((128, NFAR * RANK), BF),
+            pltpu.VMEM((FAR_UNROLL, 128, NFAR * RANK), BF),
             pltpu.VMEM((1, 2048), jnp.int32),
             pltpu.SMEM((NNEAR, CPD), jnp.int32),
             pltpu.SMEM((NFAR, CPD), jnp.int32),

time: 57.9 us -> 52 us (0.90)
  Pallas kernels: 57.1 us -> 51 us
    pallas_call x1, Pallas kernels: 52.6 us -> 46.4 us  [per_device(): pl.pallas_call(kernel, out_shape=(jax.ShapeDtypeStruct((64, ROWS), BF), j...]
where the time goes in v4:
time: 52 us; the launch traced here: 51.6 us
  Pallas kernels  51 us (98%)
  between operations  0.64 us (1%)
    pallas_call x1, Pallas kernels, per_device(): pl.pallas_call(kernel, out_shape=(jax.ShapeDtypeStruct((64, ROWS), BF), j...  46.4 us
    pallas_call x1, Pallas kernels, per_device(): pl.pallas_call(finish, out_shape=(jax.ShapeDtypeStruct((NRHS, ROWS), F32)...  4.57 us

profile of v4, /device:TPU:0, one launch (start us, length us, event | category | flops | bytes accessed | tf_op | source)
XLA Modules:
  0.0 51.6 jit_solution(14095033444337625880)
XLA Ops:
  0.6 46.4 %shard_map.121 = (bf16[64,6144]{1,0:T(8,128)(2,1)}, f32[8,128]{1,0:T(8,128)}) custom-call(f32[16,6144]{1,0:T(8,128)} %cur_h.1, f32[16,6144]{1,0:T(8,128)} %prev_h.1, f32[16,16]{1,0:T(8,128)} %pc_h.1, f32[48,128]{1,0:T(8,128)} %bitcast.10, bf16[384,128,128]{2,1,0:T(8,128)(2,1)} %bitcast.7, s32[8,48]{1,0:T(8,128)} %bitcast.13, bf16[1152,128]{1,0:T(8,128)(2,1)} %bitcast.9, ...), custom_call_target="tpu_custom_call" | custom-call | tf_op jit(solution)/shard_map/pallas_call | solution.py:504
  47.1 4.6 %shard_map.122 = (f32[16,6144]{1,0:T(8,128)}, f32[16,16]{1,0:T(8,128)}, f32[16,16]{1,0:T(8,128)}) custom-call(bf16[64,6144]{1,0:T(8,128)(2,1)} %get-tuple-element.5.stack_h, f32[8,128]{1,0:T(8,128)} %get-tuple-element.6.mixed_ref), custom_call_target="tpu_custom_call" | custom-call | tf_op jit(solution)/shard_map/pallas_call | solution.py:570

commit v5 on v4

--- a/solution.py
+++ b/solution.py
@@ -22,14 +22,14 @@
 ROWS = CPD * CL
 NGRP = CPD // 8
 HIGHEST = lax.Precision.HIGHEST
-PART_TILES = (4, 4, 2)
-PART_BASE = (0, 512, 1024)
+PART_TILES = (3, 4, 3)
+PART_BASE = (0, 384, 896)
 PER_TILE = 5
 ORDERS = ((0, 1, 2), (2, 0, 1), (1, 2, 0))
 OFFSETS = (2, 1, 3)
 RELAY_UP, RELAY_DOWN = (0, 3), (1,)
-XC = [(dx, dc) for dx in range(4) for dc in range(2) if dx or dc]
-YZ = [(dy, dz) for dy in range(4) for dz in range(4) if dy or dz]
+XC = [(2, 0), (2, 1), (1, 0), (3, 0), (1, 1), (3, 1), (0, 1)]
+YZ = sorted([(dy, dz) for dy in range(4) for dz in range(4) if dy or dz], key=lambda o: -(min(o[0], 4 - o[0]) + min(o[1], 4 - o[1])))
 TILES = 1280
 FAR_UNROLL = 6
 NEAR_CHUNKS = 6
@@ -322,7 +322,7 @@
     def near_chunk(n):
         rows_per = CPD // NEAR_CHUNKS
         near_loads[n].wait()
-        lax.fori_loop(n * rows_per, (n + 1) * rows_per, near_step, 0, unroll=4)
+        lax.fori_loop(n * rows_per, (n + 1) * rows_per, near_step, 0, unroll=8)
 
     def forward3(k2):
         for p in range(3):
@@ -350,10 +350,10 @@
     t = lax.broadcasted_iota(jnp.int32, (1, 2048), 1) >> 4
     sx, sy, sz, sc = t & 3, (t >> 2) & 3, (t >> 4) & 3, t >> 6
     tile = (local * 13) >> 6
-    at_a = (((sc * 4 + sz) * 4 + sy) * 4 + sx) * 4 + tile
-    at_b = PART_BASE[1] + (((sc * 4 + sy) * 4 + sx) * 4 + sz) * 4 + tile - 4
-    at_c = PART_BASE[2] + (((sc * 4 + sx) * 4 + sz) * 4 + sy) * 2 + tile - 8
-    at = jnp.where(tile < 4, at_a, jnp.where(tile < 8, at_b, at_c))
+    at_a = (((sc * 4 + sz) * 4 + sy) * 4 + sx) * 3 + tile
+    at_b = PART_BASE[1] + (((sc * 4 + sy) * 4 + sx) * 4 + sz) * 4 + tile - 3
+    at_c = PART_BASE[2] + (((sc * 4 + sx) * 4 + sz) * 4 + sy) * 3 + tile - 7
+    at = jnp.where(tile < 3, at_a, jnp.where(tile < 7, at_b, at_c))
     turn = (128 - (local - tile * PER_TILE) * RANK) & 127
     addr_v[...] = jnp.clip(at, 0, TILES - 1) * 128 + turn
     addr_copy = pltpu.make_async_copy(addr_v, addr_s, smem_sem.at[2])
@@ -451,11 +451,13 @@
     lane_id = lax.broadcasted_iota(jnp.int32, (16, 128), 1)
     jj, cj, cc, proj = mixed[:, 0:16], mixed[:, 16:32], mixed[:, 32:48], mixed[:, 48:64]
     proj_ref[...] = proj
-    both = tn(proj, mixed[:, 16:48], HIGHEST)
-    gram = jj - both[:, 0:16] - nn(cj.T - both[:, 16:32], proj, HIGHEST)
+    left = jnp.concatenate([proj, cj], axis=0)
+    right = jnp.concatenate([cj - nn(cc, proj, HIGHEST), proj], axis=0)
+    gram = jj - tn(left, right, HIGHEST)
 
     eye = (lane_id[:, 0:16] == row_id[:, 0:16]).astype(F32)
-    m = jnp.concatenate([gram, eye, jnp.zeros((16, 96), F32)], axis=1)
+    minus = -proj.T
+    m = jnp.concatenate([gram, eye, eye, minus, minus, jnp.zeros((16, 48), F32)], axis=1)
     for k in range(16):
         pivot_row = jnp.broadcast_to(m[k : k + 1, :], (16, 128))
         pivot = m[k : k + 1, k : k + 1]
@@ -465,17 +467,8 @@
     m = m / jnp.sqrt(d)
     upper = jnp.where(lane_id[:, 0:16] >= row_id[:, 0:16], m[:, 0:16], 0.0)
     tri_ref[...] = upper.T
-    inverse = m[:, 16:32]
-    m2 = -nt(inverse, proj, HIGHEST)
-    m1_hi, m1_lo = split(inverse)
-    m2_hi, m2_lo = split(m2)
-    lhs = jnp.concatenate(
-        [
-            jnp.concatenate([m1_hi, m1_hi, m2_hi, m2_hi], axis=1),
-            jnp.concatenate([m1_lo, m1_lo, m2_lo, m2_lo], axis=1),
-        ],
-        axis=0,
-    )
+    hi, lo = split(m[:, 16:80])
+    lhs = jnp.concatenate([hi, lo], axis=0)
 
     def out_step(c, _):
         cols = pl.ds(pl.multiple_of(c * 1024, 1024), 1024)

time: 52 us -> 51 us (0.981)
  Pallas kernels: 51 us -> 50.1 us
    pallas_call x1, Pallas kernels: 46.4 us -> 45.7 us  [per_device(): pl.pallas_call(kernel, out_shape=(jax.ShapeDtypeStruct((64, ROWS), BF), j...]
where the time goes in v5:
time: 51 us; the launch traced here: 50.7 us
  Pallas kernels  50.1 us (98%)
  between operations  0.64 us (1%)
    pallas_call x1, Pallas kernels, per_device(): pl.pallas_call(kernel, out_shape=(jax.ShapeDtypeStruct((64, ROWS), BF), j...  45.7 us
    pallas_call x1, Pallas kernels, per_device(): pl.pallas_call(finish, out_shape=(jax.ShapeDtypeStruct((NRHS, ROWS), F32)...  4.4 us

profile of v5, /device:TPU:0, one launch (start us, length us, event | category | flops | bytes accessed | tf_op | source)
XLA Modules:
  0.0 50.7 jit_solution(7176238253794161231)
XLA Ops:
  0.6 45.7 %shard_map.121 = (bf16[64,6144]{1,0:T(8,128)(2,1)}, f32[8,128]{1,0:T(8,128)}) custom-call(f32[16,6144]{1,0:T(8,128)} %cur_h.1, f32[16,6144]{1,0:T(8,128)} %prev_h.1, f32[16,16]{1,0:T(8,128)} %pc_h.1, f32[48,128]{1,0:T(8,128)} %bitcast.10, bf16[384,128,128]{2,1,0:T(8,128)(2,1)} %bitcast.7, s32[8,48]{1,0:T(8,128)} %bitcast.13, bf16[1152,128]{1,0:T(8,128)(2,1)} %bitcast.9, ...), custom_call_target="tpu_custom_call" | custom-call | tf_op jit(solution)/shard_map/pallas_call | solution.py:497
  46.3 4.4 %shard_map.122 = (f32[16,6144]{1,0:T(8,128)}, f32[16,16]{1,0:T(8,128)}, f32[16,16]{1,0:T(8,128)}) custom-call(bf16[64,6144]{1,0:T(8,128)(2,1)} %get-tuple-element.5.stack_h, f32[8,128]{1,0:T(8,128)} %get-tuple-element.6.mixed_ref), custom_call_target="tpu_custom_call" | custom-call | tf_op jit(solution)/shard_map/pallas_call | solution.py:563

commit v6 on v5

--- a/solution.py
+++ b/solution.py
@@ -95,6 +95,12 @@
         d = (me + off) % 128
         return (d // 16, d % 16)
 
+    peers = [at_xc(dx, dc) for dx, dc in XC] + [at_yz(dy, dz) for dy, dz in YZ]
+    peers += [neighbour(1), neighbour(127)]
+    barrier = pltpu.get_barrier_semaphore()
+    for d in peers:
+        pl.semaphore_signal(barrier, inc=1, device_id=d, device_id_type=MESH)
+
     loads = {}
     for n, (name, src, dst) in enumerate(
         (
@@ -112,12 +118,6 @@
         copy = pltpu.make_async_copy(near_h.at[part], near_v.at[part], near_sem.at[n])
         copy.start()
         near_loads.append(copy)
-
-    peers = [at_xc(dx, dc) for dx, dc in XC] + [at_yz(dy, dz) for dy, dz in YZ]
-    peers += [neighbour(1), neighbour(127)]
-    barrier = pltpu.get_barrier_semaphore()
-    for d in peers:
-        pl.semaphore_signal(barrier, inc=1, device_id=d, device_id_type=MESH)
 
     loads["cur"].wait()
 
@@ -437,10 +437,10 @@
 
 
 def finish(stack_h, mixed_ref, out_h, proj_ref, tri_ref, stack, out_v, load_sem, out_sem):
-    half = ROWS // 2
+    third = ROWS // 3
     loads = []
-    for n in range(2):
-        part = pl.ds(n * half, half)
+    for n in range(3):
+        part = pl.ds(n * third, third)
         loads.append(
             pltpu.make_async_copy(stack_h.at[:, part], stack.at[:, part], load_sem.at[n])
         )
@@ -477,10 +477,10 @@
         return 0
 
     stores = []
-    for n in range(2):
-        part = pl.ds(n * half, half)
+    for n in range(3):
+        part = pl.ds(n * third, third)
         loads[n].wait()
-        lax.fori_loop(n * 3, n * 3 + 3, out_step, 0, unroll=3)
+        lax.fori_loop(n * 2, n * 2 + 2, out_step, 0, unroll=2)
         stores.append(pltpu.make_async_copy(out_v.at[:, part], out_h.at[:, part], out_sem.at[n]))
         stores[n].start()
     for copy in stores:
@@ -572,8 +572,8 @@
         scratch_shapes=[
             pltpu.VMEM((64, ROWS), BF),
             pltpu.VMEM((NRHS, ROWS), F32),
-            dma((2,)),
-            dma((2,)),
+            dma((3,)),
+            dma((3,)),
         ],
     )(stack, mixed)
 

time: 51 us -> 51.2 us (level)
  no operation moved by 1% of the time
where the time goes in v6:
time: 51.2 us; the launch traced here: 50.8 us
  Pallas kernels  50.2 us (98%)
  between operations  0.64 us (1%)
    pallas_call x1, Pallas kernels, per_device(): pl.pallas_call(kernel, out_shape=(jax.ShapeDtypeStruct((64, ROWS), BF), j...  45.7 us
    pallas_call x1, Pallas kernels, per_device(): pl.pallas_call(finish, out_shape=(jax.ShapeDtypeStruct((NRHS, ROWS), F32)...  4.52 us

profile of v6, /device:TPU:0, one launch (start us, length us, event | category | flops | bytes accessed | tf_op | source)
XLA Modules:
  0.0 50.8 jit_solution(1967934866285139368)
XLA Ops:
  0.6 45.7 %shard_map.121 = (bf16[64,6144]{1,0:T(8,128)(2,1)}, f32[8,128]{1,0:T(8,128)}) custom-call(f32[16,6144]{1,0:T(8,128)} %cur_h.1, f32[16,6144]{1,0:T(8,128)} %prev_h.1, f32[16,16]{1,0:T(8,128)} %pc_h.1, f32[48,128]{1,0:T(8,128)} %bitcast.10, bf16[384,128,128]{2,1,0:T(8,128)(2,1)} %bitcast.7, s32[8,48]{1,0:T(8,128)} %bitcast.13, bf16[1152,128]{1,0:T(8,128)(2,1)} %bitcast.9, ...), custom_call_target="tpu_custom_call" | custom-call | tf_op jit(solution)/shard_map/pallas_call | solution.py:497
  46.3 4.5 %shard_map.122 = (f32[16,6144]{1,0:T(8,128)}, f32[16,16]{1,0:T(8,128)}, f32[16,16]{1,0:T(8,128)}) custom-call(bf16[64,6144]{1,0:T(8,128)(2,1)} %get-tuple-element.5.stack_h, f32[8,128]{1,0:T(8,128)} %get-tuple-element.6.mixed_ref), custom_call_target="tpu_custom_call" | custom-call | tf_op jit(solution)/shard_map/pallas_call | solution.py:563
